TPU v7x, 32 devices: a whole 2x2x4 slice. The times are simulated.
32 devices in a mesh: blk: 8 (over z, x), rep: 4 (over y, core).
Axes of the slice: x: 2, y: 2, z: 4, core: 2. Of those that a mesh axis runs over, the one named last changes fastest.
Arguments:
- features: bfloat16 [32768, 128], P(('blk', 'rep')), may hold values from -6 to 6
- weight: bfloat16 [128, 512], replicated, may hold values from -0.5 to 0.5
- bias: float32 [512], replicated, may hold values from -3 to 3
- tile_values: bfloat16 [32768, 4096], P(('blk', 'rep')), may hold values from -0.125 to 0.125
- tile_cols: int32 [256, 32], P(('blk', 'rep')), may hold values from 0 to 95, as said below
- tile_counts: int32 [256], P(('blk', 'rep')), may hold values from 1 to 32, as said below
- out_grad: bfloat16 [32768, 512], P(('blk', 'rep')), may hold values from -6 to 6
Outputs:
- activations: bfloat16 [32768, 512], P(('blk', 'rep'))
- feature_grad: float32 [32768, 128], P(('blk', 'rep'))
- weight_grad: float32 [128, 512], replicated
- bias_grad: float32 [512], replicated
Inputs may be any that keep to these rules, and one draw needn't show every extreme that they name: `tile_cols`: within one row tile the 32 entries are different. `tile_counts`: slots 0 to count - 1 of a row tile are live.
All inputs are finite; a program needn't handle non-finite values.
Results may differ from a plain program's by a relative error of at most 0.0059.
Values may be sent and summed in bfloat16 or wider, within the bound.
A program may use at most 128 MiB of HBM per device.

v0:
```python
import math

import jax
import jax.numpy as jnp
from jax import lax
from jax.sharding import PartitionSpec as P

TILE = 128
REACH = 1
SLOTS = 32


def passed_along(value, axis, steps):
    count = lax.axis_size(axis)
    pairs = [(source, (source + steps) % count) for source in range(count)]
    return lax.ppermute(value, axis, pairs)


def gelu_parts(pre_act):
    inner = 0.7978845608028654 * (pre_act + 0.044715 * pre_act * pre_act * pre_act)
    tangent = jnp.tanh(inner)
    value_part = 0.5 * pre_act * (1.0 + tangent)
    slope = 0.5 * (1.0 + tangent) + 0.5 * pre_act * (
        1.0 - tangent * tangent
    ) * 0.7978845608028654 * (1.0 + 0.134145 * pre_act * pre_act)
    return (value_part, slope)


def on_device(features, weight, bias, tile_values, tile_cols, tile_counts, out_grad):
    rows_dev, in_dim = features.shape
    row_tiles = rows_dev // TILE
    group_size = lax.axis_size("rep")
    block_rows = rows_dev * group_size
    nodes = block_rows * lax.axis_size("blk")
    offsets = list(range(-REACH, REACH + 1))
    pieces = []
    for offset_now in offsets:
        if offset_now == 0:
            pieces.append(features)
        else:
            pieces.append(passed_along(features, "blk", -offset_now))
    stacked = jnp.stack(pieces)
    window = lax.all_gather(stacked, "rep", axis=1, tiled=True).reshape(-1, in_dim)
    window_tiles = window.reshape(-1, TILE, in_dim)
    is_live = jnp.arange(SLOTS)[None, :] < tile_counts[:, None]
    gathered = window_tiles[tile_cols]
    gathered = jnp.where(is_live[:, :, None, None], gathered, jnp.zeros((), gathered.dtype))
    gathered = gathered.reshape(row_tiles, SLOTS * TILE, in_dim)
    values = tile_values.reshape(row_tiles, TILE, SLOTS * TILE)
    summed = jnp.einsum(
        "rik,rkf->rif", values, gathered, preferred_element_type=jnp.float32
    ).reshape(rows_dev, in_dim)
    aggregated = summed.astype(jnp.bfloat16)
    pre_act = jnp.dot(aggregated, weight, preferred_element_type=jnp.float32) + bias
    value_part, slope = gelu_parts(pre_act)
    activations = value_part.astype(jnp.bfloat16)
    pre_grad = (out_grad.astype(jnp.float32) * slope).astype(jnp.bfloat16)
    factor = 1.0 / math.sqrt(nodes)
    local_weight = (
        lax.dot_general(
            aggregated, pre_grad, (((0,), (0,)), ((), ())), preferred_element_type=jnp.float32
        )
        * factor
    )
    local_bias = jnp.sum(pre_grad.astype(jnp.float32), axis=0) * factor
    weight_grad, bias_grad = lax.psum((local_weight, local_bias), ("blk", "rep"))
    row_grad = lax.dot_general(
        pre_grad, weight, (((1,), (1,)), ((), ())), preferred_element_type=jnp.float32
    ).astype(jnp.bfloat16)
    grad_tiles = row_grad.reshape(row_tiles, TILE, in_dim)
    partial_value = jnp.einsum(
        "rik,rif->rkf", values, grad_tiles, preferred_element_type=jnp.float32
    )
    partial_value = partial_value.reshape(row_tiles, SLOTS, TILE, in_dim)
    partial_value = jnp.where(
        is_live[:, :, None, None], partial_value, jnp.zeros((), partial_value.dtype)
    )
    window_count = len(offsets) * block_rows // TILE
    placed = (
        jnp.zeros((window_count, TILE, in_dim), jnp.float32)
        .at[tile_cols.reshape(-1)]
        .add(partial_value.reshape(-1, TILE, in_dim))
    )
    terms = placed.reshape(len(offsets), block_rows, in_dim)
    block_total = terms[REACH]
    for position, offset_now in enumerate(offsets):
        if offset_now != 0:
            block_total = block_total + passed_along(
                terms[position].astype(jnp.bfloat16), "blk", offset_now
            ).astype(jnp.float32)
    feature_grad = lax.psum_scatter(block_total, "rep", scatter_dimension=0, tiled=True)
    return (activations, feature_grad, weight_grad, bias_grad)


def solution(mesh):
    in_specs = (
        P(("blk", "rep"), None),
        P(),
        P(),
        P(("blk", "rep"), None),
        P(("blk", "rep"), None),
        P(("blk", "rep")),
        P(("blk", "rep"), None),
    )
    out_specs = (P(("blk", "rep"), None), P(("blk", "rep"), None), P(), P())
    return jax.shard_map(
        on_device, mesh=mesh, in_specs=in_specs, out_specs=out_specs, check_vma=False
    )
```

profile of v0, /device:TPU:0, one launch (start us, length us, event | category | flops | bytes accessed | tf_op | source)
XLA Modules:
  0.0 377.3 jit_solution(3224412741423206492)
XLA Ops:
  7.2 3.0 collective-permute-start
  10.2 3.1 collective-permute-start.1
  13.3 8.4 %collective-permute-done = bf16[1024,128]{1,0:T(8,128)(2,1)S(1)} collective-permute-done((bf16[1024,128]{1,0:T(8,128)(2,1)}, bf16[1024,128]{1,0:T(8,128)(2,1)S(1)}, u32[]{:S(2)}, u32[]{:S(2)}) %collective-permute-start) | collective-permute-done | bytes 262176 | tf_op jit(solution)/shard_map/ppermute | solution.py:16
  21.7 2.1 collective-permute-done.1
  23.8 1.9 pad_maximum_fusion
  28.4 26.1 %all-gather.2.cloned.1.call-done = bf16[3,4096,128]{2,1,0:T(8,128)(2,1)} async-done(((bf16[3,1024,128]{2,1,0:T(8,128)(2,1)}), bf16[3,4096,128]{2,1,0:T(8,128)(2,1)}) %all-gather.2.cloned.1.call-update) | async-done | bytes 3145744 | tf_op jit(solution)/shard_map/all_gather | solution.py:43
  54.5 10.5 %gather_fusion = bf16[256,128,128]{2,1,0:T(8,128)(2,1)} fusion(bf16[96,128,128]{2,1,0:T(8,128)(2,1)} %bitcast.40, s32[1024]{0:T(1024)S(1)} %pad_clamp_fusion), kind=kCustom, calls=%fused_computation | custom fusion | bytes 16778240 | tf_op jit(solution)/shard_map/gather | solution.py:46
  65.0 16.3 %bitcast_select_fusion = bf16[8,4096,128]{2,1,0:T(8,128)(2,1)S(1)} fusion(pred[8,4096]{1,0:T(8,128)(4,1)S(1)} %broadcast_bitcast_fusion, bf16[8,4096,128]{2,1,0:T(8,128)(2,1)} %bitcast.39), kind=kLoop, calls=%fused_computation.3 | loop fusion | flops 4194304 | bytes 16809984 | tf_op jit(solution)/shard_map/jit(_where)/select_n | solution.py:47
  81.4 5.8 %convolution_convert_fusion = bf16[8,128,128]{1,2,0:T(8,128)(2,1)S(1)} fusion(bf16[8,128,4096]{2,1,0:T(8,128)(2,1)} %bitcast.35, bf16[8,4096,128]{2,1,0:T(8,128)(2,1)S(1)} %bitcast_select_fusion), kind=kOutput, calls=%fused_computation.18 | convolution fusion | flops 1073872896 | bytes 17039360 | tf_op jit(solution)/shard_map/rik,rkf->rif/dot_general | solution.py:50
  87.2 2.7 convert_reduce_fusion
  91.0 8.1 %convolution_bitcast_fusion = f32[8,4096,128]{1,2,0:T(8,128)} fusion(bf16[8,128,128]{2,1,0:T(8,128)(2,1)S(1)} %bitcast.41, bf16[8,128,4096]{2,1,0:T(8,128)(2,1)S(1)} %bitcast.38), kind=kOutput, calls=%fused_computation.2 | convolution fusion | flops 1073741824 | bytes 25427968 | tf_op jit(solution)/shard_map/rik,rif->rkf/dot_general | solution.py:71
  99.1 17.4 %copy.14 = f32[8,4096,128]{2,1,0:T(8,128)} copy(f32[8,4096,128]{1,2,0:T(8,128)} %convolution_bitcast_fusion) | data formatting | bytes 33554432 | tf_op jit(solution)/shard_map/rik,rif->rkf/dot_general | solution.py:71
  116.6 11.6 %broadcast_select_fusion = f32[256,128,128]{2,1,0:T(8,128)} fusion(f32[256,128,128]{2,1,0:T(8,128)} %bitcast.34, pred[256]{0:T(512)(128)(4,1)S(1)} %lt.47), kind=kLoop, calls=%fused_computation.4 | loop fusion | flops 4194304 | bytes 33554688 | tf_op jit(solution)/shard_map/jit(_where)/select_n | solution.py:75
  128.2 3.4 broadcast_in_dim.45
  131.6 52.6 %scatter_fusion = f32[96,128,128]{2,1,0:T(8,128)} fusion(f32[96,128,128]{2,1,0:T(8,128)} %broadcast_in_dim.45, s32[256]{0:T(256)S(1)} %bitcast.47, f32[256,128,128]{2,1,0:T(8,128)} %broadcast_select_fusion), kind=kCustom, calls=%fused_computation.1 | custom fusion | flops 4194304 | bytes 50332672 | tf_op jit(solution)/shard_map/scatter-add | solution.py:82
  184.3 3.5 convert.4
  189.2 4.1 %collective-permute-start.2 = (bf16[4096,128]{1,0:T(8,128)(2,1)}, bf16[4096,128]{1,0:T(8,128)(2,1)}, u32[]{:S(2)}, u32[]{:S(2)}) collective-permute-start(bf16[4096,128]{1,0:T(8,128)(2,1)} %bitcast.14), channel_id=1, source_target_pairs={{0,28},{4,0},{8,4},{12,8},{16,12},{20,16},{24,20},{28,24},{1,29},{... | collective-permute-start | bytes 3145736 | tf_op jit(solution)/shard_map/ppermute | solution.py:16
  193.3 1.7 slice.19
  196.1 41.6 %collective-permute-done.2 = bf16[4096,128]{1,0:T(8,128)(2,1)} collective-permute-done((bf16[4096,128]{1,0:T(8,128)(2,1)}, bf16[4096,128]{1,0:T(8,128)(2,1)}, u32[]{:S(2)}, u32[]{:S(2)}) %collective-permute-start.2) | collective-permute-done | bytes 1048608 | tf_op jit(solution)/shard_map/ppermute | solution.py:16
  237.8 3.4 fusion.7
  241.2 39.4 %psum.15 = f32[512]{0:T(512)} all-reduce(f32[512]{0:T(512)S(1)} %broadcast_multiply_fusion), channel_id=1, replica_groups=mesh['blk'=8,'rep'=4] {'blk','rep'}, use_global_device_ids=true, to_apply=%region_4.5 | all-reduce | flops 512 | bytes 4096 | tf_op jit(solution)/shard_map/psum | solution.py:66
  280.7 54.8 %all-reduce.2.cloned.1.call-done = f32[128,512]{1,0:T(8,128)} async-done(((f32[128,512]{1,0:T(8,128)}), f32[128,512]{1,0:T(8,128)}) %all-reduce.2.cloned.1.call-update) | async-done | bytes 262160 | tf_op jit(solution)/shard_map/psum | solution.py:66
  335.5 33.6 %reduce-scatter.2.cloned.1.call-done = f32[1024,128]{1,0:T(8,128)} async-done(((f32[4096,128]{1,0:T(8,128)}), f32[1024,128]{1,0:T(8,128)}) %reduce-scatter.2.cloned.1.call-update) | async-done | bytes 524304 | tf_op jit(solution)/shard_map/reduce_scatter | solution.py:91
  369.1 1.7 copy.18
  (34 shorter events, 6.3 us)
Async XLA Ops:
  7.2 80.0 %copy-start = (bf16[128,512]{1,0:T(8,128)(2,1)S(1)}, bf16[128,512]{1,0:T(8,128)(2,1)}, u32[]{:S(2)}) copy-start(bf16[128,512]{1,0:T(8,128)(2,1)} %param.8) | copy-start | bytes 393220
  7.2 47.3 %all-gather.2.cloned.1.call-start = ((), (), s32[]{:S(2)}) async-start(), calls=%async_computation.1 | async-start | bytes 3932160 | tf_op jit(solution)/shard_map/all_gather | solution.py:43
  7.2 14.5 %collective-permute-start = (bf16[1024,128]{1,0:T(8,128)(2,1)}, bf16[1024,128]{1,0:T(8,128)(2,1)S(1)}, u32[]{:S(2)}, u32[]{:S(2)}) collective-permute-start(bf16[1024,128]{1,0:T(8,128)(2,1)} %param.7), channel_id=1, source_target_pairs={{0,4},{4,8},{8,12},{12,16},{16,20},{20,24},{24,28},{28,0},{1,5},{5... | collective-permute-start | bytes 786440 | tf_op jit(solution)/shard_map/ppermute | solution.py:16
  10.2 13.6 %collective-permute-start.1 = (bf16[1024,128]{1,0:T(8,128)(2,1)}, bf16[1024,128]{1,0:T(8,128)(2,1)S(1)}, u32[]{:S(2)}, u32[]{:S(2)}) collective-permute-start(bf16[1024,128]{1,0:T(8,128)(2,1)} %param.7), channel_id=1, source_target_pairs={{0,28},{4,0},{8,4},{12,8},{16,12},{20,16},{24,20},{28,24},{1,29},{... | collective-permute-start | bytes 786440 | tf_op jit(solution)/shard_map/ppermute | solution.py:16
  25.8 309.8 %all-reduce.2.cloned.1.call-start = ((), (), s32[]{:S(2)}) async-start(), calls=%async_computation.3 | async-start | bytes 524288 | tf_op jit(solution)/shard_map/psum | solution.py:66
  81.3 5.9 %copy-start.2 = (bf16[1024,512]{1,0:T(8,128)(2,1)S(1)}, bf16[1024,512]{1,0:T(8,128)(2,1)}, u32[]{:S(2)}) copy-start(bf16[1024,512]{1,0:T(8,128)(2,1)} %param.13) | copy-start | bytes 3145732
  81.3 5.9 %copy-start.3 = (f32[512]{0:T(512)S(1)}, f32[512]{0:T(512)}, u32[]{:S(2)}) copy-start(f32[512]{0:T(512)} %param.9) | copy-start | bytes 6148
  87.2 3.2 slice-start
  87.2 3.8 %slice-start.1 = ((s8[8388608]{0:T(1024)(128)(4,1)}), s8[4194304]{0:T(1024)(128)(4,1)S(1)}, s32[]{:S(2)}) async-start(s8[8388608]{0:T(1024)(128)(4,1)} %bitcast.36), calls=%async_computation.5 | async-start | bytes 8388608
  189.2 48.6 %collective-permute-start.2 = (bf16[4096,128]{1,0:T(8,128)(2,1)}, bf16[4096,128]{1,0:T(8,128)(2,1)}, u32[]{:S(2)}, u32[]{:S(2)}) collective-permute-start(bf16[4096,128]{1,0:T(8,128)(2,1)} %bitcast.14), channel_id=1, source_target_pairs={{0,28},{4,0},{8,4},{12,8},{16,12},{20,16},{24,20},{28,24},{1,29},{... | collective-permute-start | bytes 3145736 | tf_op jit(solution)/shard_map/ppermute | solution.py:16
  193.3 44.5 %collective-permute-start.3 = (bf16[4096,128]{1,0:T(8,128)(2,1)}, bf16[4096,128]{1,0:T(8,128)(2,1)}, u32[]{:S(2)}, u32[]{:S(2)}) collective-permute-start(bf16[4096,128]{1,0:T(8,128)(2,1)} %bitcast.15), channel_id=1, source_target_pairs={{0,4},{4,8},{8,12},{12,16},{16,20},{20,24},{24,28},{28,0},{1,5},{5... | collective-permute-start | bytes 3145736 | tf_op jit(solution)/shard_map/ppermute | solution.py:16
  196.1 174.7 %copy-start.1 = (bf16[128,512]{1,0:T(8,128)(2,1)S(1)}, bf16[128,512]{1,0:T(8,128)(2,1)}, u32[]{:S(2)}) copy-start(bf16[128,512]{1,0:T(8,128)(2,1)} %param.8) | copy-start | bytes 393220
  196.1 173.0 %reduce-scatter.2.cloned.1.call-start = ((), (), s32[]{:S(2)}) async-start(), calls=%async_computation.2 | async-start | bytes 2621440 | tf_op jit(solution)/shard_map/reduce_scatter | solution.py:91
Sparse Core Ops, SparseCore 0:
  25.9 28.5 all-gather.1
  196.2 139.2 all-reduce.1
  338.6 30.4 reduce-scatter.1
where the time goes:
time: 379 us; the launch traced here: 377 us
  waiting for transfers between devices  167 us (44%)
  other arithmetic  90.8 us (24%)
  blocking collectives  39.4 us (10%)
  local copies, waits for them, and re-layouts  38.1 us (10%)
  matrix products  18.1 us (5%)
  between operations  13.9 us (4%)
  starting transfers between devices  10.3 us (3%)
    psum x1, waiting for transfers between devices, on_device(): lax.psum((local_weight, local_bias), ('blk', 'rep'))  54.8 us
    scatter-add x1, other arithmetic, on_device(): placed = jnp.zeros((window_count, TILE, in_dim), jnp.float32).at[tile_col...  52.6 us
    ppermute x4, waiting for transfers between devices, passed_along(): return lax.ppermute(value, axis, pairs)  52.1 us
    psum x1, blocking collectives, on_device(): lax.psum((local_weight, local_bias), ('blk', 'rep'))  39.4 us
    reduce_scatter x1, waiting for transfers between devices, on_device(): lax.psum_scatter(block_total, 'rep', scatter_dimension=0, tiled=True)  33.6 us
    all_gather x1, waiting for transfers between devices, on_device(): lax.all_gather(stacked, 'rep', axis=1, tiled=True).reshape(-1, in_dim)  26.1 us
    dot_general x1, local copies, waits for them, and re-layouts, on_device(): jnp.einsum('rik,rif->rkf', values, grad_tiles, preferred_element_type=jnp...  17.4 us
    select_n x1, other arithmetic, on_device(): jnp.where(is_live[:, :, None, None], gathered, jnp.zeros((), gathered.dty...  16.3 us
  transfers between devices with their start and end apart: 7, of which 6 were waited for; matrix products, arithmetic and copies ran while one was open for 2% of the time, Pallas kernels for 0%

commit v1 on v0

v1 whole, which is shorter than its diff:
```python
import functools
import math

import jax
import jax.numpy as jnp
from jax import lax
from jax.experimental import pallas as pl
from jax.experimental.pallas import tpu as pltpu
from jax.sharding import PartitionSpec as P

TILE = 128
SIDES = 3
GROUP = 4
CHUNKS = 4
SPAN = 8
BIAS_ROWS = 8
MESH = pl.DeviceIdType.MESH
VMEM = pl.BlockSpec(memory_space=pltpu.VMEM)
SMEM = pl.BlockSpec(memory_space=pltpu.SMEM)
ANY = pl.BlockSpec(memory_space=pl.ANY)
LIMIT = 56 * 1024 * 1024


def partners():
    rep = lax.axis_index("rep")
    return rep + 1 - 2 * (rep % 2), (rep + 2) % GROUP


def gather_kernel(count, own_ref, win_ref, own_sem, blk_send, blk_recv, far_send, far_recv,
                  near_send, near_recv):
    blk, rep = lax.axis_index("blk"), lax.axis_index("rep")
    near, far = partners()
    across = (near + 2) % GROUP
    before, after = (blk + count - 1) % count, (blk + 1) % count
    rows = own_ref.shape[0] // CHUNKS

    barrier = pltpu.get_barrier_semaphore()
    for device in ((before, rep), (after, rep), (blk, near), (blk, far)):
        pl.semaphore_signal(barrier, inc=1, device_id=device, device_id_type=MESH)
    pl.semaphore_wait(barrier, 4)

    def part(side, member, chunk):
        return win_ref.at[side, member, pl.ds(chunk * rows, rows)]

    def remote(source, target, send, recv, device):
        return pltpu.make_async_remote_copy(
            src_ref=source, dst_ref=target, send_sem=send, recv_sem=recv,
            device_id=device, device_id_type=MESH)

    def to_blk(which, chunk):
        side, device = ((0, (after, rep)), (2, (before, rep)))[which]
        return remote(own_ref.at[pl.ds(chunk * rows, rows)], part(side, rep, chunk),
                      blk_send.at[which, chunk], blk_recv.at[which, chunk], device)

    def to_far(side, chunk):
        source = own_ref.at[pl.ds(chunk * rows, rows)] if side == 1 else part(side, rep, chunk)
        return remote(source, part(side, rep, chunk), far_send.at[side, chunk],
                      far_recv.at[side, chunk], (blk, far))

    def to_near(side, whose, chunk):
        member = (rep, far)[whose]
        source = part(side, member, chunk)
        if side == 1 and whose == 0:
            source = own_ref.at[pl.ds(chunk * rows, rows)]
        return remote(source, part(side, member, chunk), near_send.at[side, whose, chunk],
                      near_recv.at[side, whose, chunk], (blk, near))

    started = []

    def start(copy):
        copy.start()
        started.append(copy)
        return copy

    local = pltpu.make_async_copy(own_ref, win_ref.at[1, rep], own_sem)
    blk_copies, far_copies, near_copies = {}, {}, {}
    for chunk in range(CHUNKS):
        for which in range(2):
            blk_copies[which, chunk] = start(to_blk(which, chunk))
        far_copies[1, chunk] = start(to_far(1, chunk))
    for chunk in range(CHUNKS):
        near_copies[1, 0, chunk] = start(to_near(1, 0, chunk))
    local.start()
    for chunk in range(CHUNKS):
        for which in range(2):
            blk_copies[which, chunk].wait_recv()
            side = (0, 2)[which]
            far_copies[side, chunk] = start(to_far(side, chunk))
            near_copies[side, 0, chunk] = start(to_near(side, 0, chunk))
    for side in (1, 0, 2):
        for chunk in range(CHUNKS):
            far_copies[side, chunk].wait_recv()
            near_copies[side, 1, chunk] = start(to_near(side, 1, chunk))
    for copy in near_copies.values():
        copy.wait_recv()
    for copy in started:
        copy.wait_send()
    local.wait()


def gather(features):
    rows, width = features.shape
    dma = pltpu.SemaphoreType.DMA
    return pl.pallas_call(
        functools.partial(gather_kernel, lax.axis_size("blk")),
        out_shape=jax.ShapeDtypeStruct((SIDES, GROUP, rows, width), features.dtype),
        in_specs=[VMEM],
        out_specs=VMEM,
        scratch_shapes=[
            dma, dma((2, CHUNKS)), dma((2, CHUNKS)), dma((SIDES, CHUNKS)), dma((SIDES, CHUNKS)),
            dma((SIDES, 2, CHUNKS)), dma((SIDES, 2, CHUNKS)),
        ],
        compiler_params=pltpu.CompilerParams(
            collective_id=0, has_side_effects=True, vmem_limit_bytes=LIMIT),
        name="gather_window",
    )(features)


def gelu_parts(pre_act):
    inner = 0.7978845608028654 * (pre_act + 0.044715 * pre_act * pre_act * pre_act)
    tangent = jnp.tanh(inner)
    half = 0.5 * (1.0 + tangent)
    value_part = pre_act * half
    slope = half + 0.5 * pre_act * (
        1.0 - tangent * tangent
    ) * 0.7978845608028654 * (1.0 + 0.134145 * pre_act * pre_act)
    return value_part, slope


def layer_kernel(factor, counts, cols, win_hbm, val_hbm, weight, bias, og_hbm, act_out, terms_out,
                 grad_out, vals, win, og, placed, agg, pre_grad, row_grad, acc, bias_sum, val_sem,
                 win_sem, og_sem):
    tiles, _, wide = vals.shape
    spans = wide // (SPAN * TILE)
    win_copy = pltpu.make_async_copy(win_hbm, win, win_sem)
    og_copy = pltpu.make_async_copy(og_hbm, og, og_sem)

    def val_copy(t):
        return pltpu.make_async_copy(val_hbm.at[pl.ds(t * TILE, TILE)], vals.at[t], val_sem.at[t])

    win_copy.start()
    for t in range(tiles):
        val_copy(t).start()
    og_copy.start()

    def clear(w, carry):
        placed[w] = jnp.zeros(placed.shape[1:], placed.dtype)
        return carry

    lax.fori_loop(0, placed.shape[0], clear, 0)
    win_copy.wait()

    def forward(t, carry):
        val_copy(t).wait()
        live = counts[t]
        acc[...] = jnp.zeros_like(acc)
        for span in range(spans):

            @pl.when(span * SPAN < live)
            def _():
                picked = []
                for k in range(SPAN):
                    tile = win[cols[t, span * SPAN + k]]
                    picked.append(jnp.where(span * SPAN + k < live, tile, jnp.zeros_like(tile)))
                acc[...] += jnp.dot(
                    vals[t, :, span * SPAN * TILE:(span + 1) * SPAN * TILE],
                    jnp.concatenate(picked, axis=0), preferred_element_type=jnp.float32)

        agg[pl.ds(pl.multiple_of(t * TILE, TILE), TILE)] = acc[...].astype(agg.dtype)
        return carry

    lax.fori_loop(0, tiles, forward, 0)
    og_copy.wait()
    bias_sum[...] = jnp.zeros_like(bias_sum)

    def dense(t, carry):
        here = pl.ds(pl.multiple_of(t * TILE, TILE), TILE)
        pre_act = jnp.dot(agg[here], weight[...], preferred_element_type=jnp.float32) + bias[...]
        value_part, slope = gelu_parts(pre_act)
        act_out[here] = value_part.astype(act_out.dtype)
        grad = (og[here].astype(jnp.float32) * slope).astype(jnp.bfloat16)
        pre_grad[here] = grad
        bias_sum[...] += jnp.sum(
            grad.astype(jnp.float32).reshape(TILE // 8, 8, grad.shape[1]), axis=0)
        row_grad[t] = lax.dot_general(
            weight[...], grad, (((1,), (1,)), ((), ())), preferred_element_type=jnp.float32
        ).astype(row_grad.dtype)
        return carry

    lax.fori_loop(0, tiles, dense, 0)
    weight_grad = lax.dot_general(
        agg[...], pre_grad[...], (((0,), (0,)), ((), ())), preferred_element_type=jnp.float32
    ) * factor
    bias_grad = jnp.sum(bias_sum[...], axis=0, keepdims=True) * factor
    members, blocks = grad_out.shape[:2]
    share = grad_out.shape[2] - BIAS_ROWS
    cut = grad_out.shape[3]
    for member in range(members):
        columns = slice(member * cut, (member + 1) * cut)
        grad_out[member, :, :share, :] = weight_grad[:, columns].reshape(blocks, share, cut)
        grad_out[member, :, share:, :] = jnp.broadcast_to(
            bias_grad[:, columns][None], (blocks, BIAS_ROWS, cut))

    def backward(t, carry):
        live = counts[t]
        for span in range(spans):

            @pl.when(span * SPAN < live)
            def _():
                terms = jnp.dot(
                    row_grad[t], vals[t, :, span * SPAN * TILE:(span + 1) * SPAN * TILE],
                    preferred_element_type=jnp.float32)
                for k in range(SPAN):
                    term = terms[:, k * TILE:(k + 1) * TILE]
                    term = jnp.where(span * SPAN + k < live, term, jnp.zeros_like(term))
                    placed[cols[t, span * SPAN + k]] += term

        return carry

    lax.fori_loop(0, tiles, backward, 0)

    def hand_on(w, carry):
        terms_out[w] = placed[w].astype(terms_out.dtype)
        return carry

    lax.fori_loop(0, placed.shape[0], hand_on, 0)


def layer(counts, cols, window, values, weight, bias, out_grad, factor, blocks):
    rows, wide = values.shape
    in_dim, out_dim = weight.shape
    tiles = rows // TILE
    window_tiles = SIDES * GROUP * tiles
    dma = pltpu.SemaphoreType.DMA
    window_shape = (window_tiles, TILE, in_dim)
    grad_shape = (GROUP, blocks, in_dim // blocks + BIAS_ROWS, out_dim // GROUP)
    return pl.pallas_call(
        functools.partial(layer_kernel, factor),
        out_shape=(
            jax.ShapeDtypeStruct((rows, out_dim), jnp.bfloat16),
            jax.ShapeDtypeStruct((window_tiles, in_dim, TILE), jnp.bfloat16),
            jax.ShapeDtypeStruct(grad_shape, jnp.float32),
        ),
        in_specs=[SMEM, SMEM, ANY, ANY, VMEM, VMEM, ANY],
        out_specs=(VMEM, VMEM, VMEM),
        scratch_shapes=[
            pltpu.VMEM((tiles, TILE, wide), jnp.bfloat16),
            pltpu.VMEM(window_shape, jnp.bfloat16),
            pltpu.VMEM((rows, out_dim), jnp.bfloat16),
            pltpu.VMEM((window_tiles, in_dim, TILE), jnp.float32),
            pltpu.VMEM((rows, in_dim), jnp.bfloat16),
            pltpu.VMEM((rows, out_dim), jnp.bfloat16),
            pltpu.VMEM((tiles, in_dim, TILE), jnp.bfloat16),
            pltpu.VMEM((TILE, in_dim), jnp.float32),
            pltpu.VMEM((8, out_dim), jnp.float32),
            dma((tiles,)), dma, dma,
        ],
        compiler_params=pltpu.CompilerParams(vmem_limit_bytes=LIMIT),
        name="layer",
    )(counts, cols, window.reshape(window_shape), values, weight, bias.reshape(1, -1), out_grad)


def reduce_kernel(count, terms, grads, out_ref, weight_out, bias_out, near_buf, far_out, far_buf,
                  blk_out, blk_buf, rep_buf, share_buf, share_out, whole, near_send, near_recv,
                  far_send, far_recv, blk_send, blk_recv, rep_send, rep_recv, share_send,
                  share_recv, back_send, back_recv, last_send, last_recv):
    blk, rep = lax.axis_index("blk"), lax.axis_index("rep")
    near, far = partners()
    across = (near + 2) % GROUP
    before, after = (blk + count - 1) % count, (blk + 1) % count
    tiles = out_ref.shape[0] // TILE
    step = tiles // CHUNKS
    f32 = jnp.float32

    barrier = pltpu.get_barrier_semaphore()
    for turn in range(1, GROUP):
        pl.semaphore_signal(
            barrier, inc=1, device_id=(blk, (rep + turn) % GROUP), device_id_type=MESH)
    for turn in range(1, count):
        pl.semaphore_signal(
            barrier, inc=1, device_id=((blk + turn) % count, rep), device_id_type=MESH)
    pl.semaphore_wait(barrier, GROUP + count - 2)

    started = []

    def start(source, target, send, recv, device):
        copy = pltpu.make_async_remote_copy(
            src_ref=source, dst_ref=target, send_sem=send, recv_sem=recv,
            device_id=device, device_id_type=MESH)
        copy.start()
        started.append(copy)
        return copy

    near_copies, far_copies, blk_copies = {}, {}, {}
    for whose, side in ((1, 0), (1, 2), (1, 1), (0, 0), (0, 2), (0, 1)):
        near_copies[side, whose] = start(
            terms.at[side, (near, across)[whose]], near_buf.at[side, whose],
            near_send.at[side, whose], near_recv.at[side, whose], (blk, near))
    rep_copies = [
        start(grads.at[(rep + turn) % GROUP], rep_buf.at[turn - 1], rep_send.at[turn - 1],
              rep_recv.at[turn - 1], (blk, (rep + turn) % GROUP))
        for turn in range(1, GROUP)
    ]

    for side in (0, 2, 1):
        near_copies[side, 1].wait_recv()
        for chunk in range(CHUNKS):
            here = pl.ds(chunk * step, step)
            far_out[side, here] = (
                terms[side, far, here].astype(f32) + near_buf[side, 1, here].astype(f32)
            ).astype(far_out.dtype)
            far_copies[side, chunk] = start(
                far_out.at[side, here], far_buf.at[side, here], far_send.at[side, chunk],
                far_recv.at[side, chunk], (blk, far))

    for copy in rep_copies:
        copy.wait_recv()
    share_out[...] = ((grads[rep] + rep_buf[0]) + rep_buf[1]) + rep_buf[2]
    share_copies = [
        start(share_out.at[(blk + turn) % count], share_buf.at[turn - 1], share_send.at[turn - 1],
              share_recv.at[turn - 1], ((blk + turn) % count, rep))
        for turn in range(1, count)
    ]

    for side in (0, 2, 1):
        near_copies[side, 0].wait_recv()
    for chunk in range(CHUNKS):
        here = pl.ds(chunk * step, step)
        for which, side in ((0, 0), (1, 2)):
            far_copies[side, chunk].wait_recv()
            blk_out[which, here] = (
                terms[side, rep, here].astype(f32) + near_buf[side, 0, here].astype(f32)
                + far_buf[side, here].astype(f32)
            ).astype(blk_out.dtype)
            blk_copies[which, chunk] = start(
                blk_out.at[which, here], blk_buf.at[which, here], blk_send.at[which, chunk],
                blk_recv.at[which, chunk], ((before, after)[which], rep))
        if chunk == CHUNKS // 2 - 1:
            for copy in share_copies:
                copy.wait_recv()
            total = share_out[blk]
            for turn in range(1, count):
                total += share_buf[turn - 1]
            whole[rep, blk] = total
            back_copies = [
                start(whole.at[rep, blk], whole.at[rep, blk], back_send.at[turn - 1],
                      back_recv.at[turn - 1], ((blk + turn) % count, rep))
                for turn in range(1, count)
            ]

    for copy in back_copies:
        copy.wait_recv()
    last_copies = [
        start(whole.at[rep], whole.at[rep], last_send.at[turn - 1], last_recv.at[turn - 1],
              (blk, (rep + turn) % GROUP))
        for turn in range(1, GROUP)
    ]

    for chunk in range(CHUNKS):
        far_copies[1, chunk].wait_recv()
        here = pl.ds(chunk * step, step)
        total = (
            terms[1, rep, here].astype(f32) + near_buf[1, 0, here].astype(f32)
            + far_buf[1, here].astype(f32)
        )
        for which in range(2):
            blk_copies[which, chunk].wait_recv()
            total += blk_buf[which, here].astype(f32)
        for k in range(step):
            out_ref[pl.ds((chunk * step + k) * TILE, TILE)] = total[k].T

    for copy in last_copies:
        copy.wait_recv()
    blocks, share = whole.shape[1], whole.shape[2] - BIAS_ROWS
    cut = whole.shape[3]
    for member in range(GROUP):
        columns = slice(member * cut, (member + 1) * cut)
        weight_out[:, columns] = whole[member, :, :share, :].reshape(blocks * share, cut)
        bias_out[:, columns] = whole[member, 0, share:share + 1, :]
    for copy in started:
        copy.wait_send()


def reduce(terms, grads, rows):
    count = lax.axis_size("blk")
    tiles, in_dim, _ = terms.shape
    tiles = tiles // (SIDES * GROUP)
    terms = terms.reshape(SIDES, GROUP, tiles, in_dim, TILE)
    _, blocks, share, cut = grads.shape
    piece = (tiles, in_dim, TILE)
    dma = pltpu.SemaphoreType.DMA
    pairs = [(SIDES, 2), (SIDES, CHUNKS), (2, CHUNKS), (GROUP - 1,), (count - 1,), (count - 1,),
             (GROUP - 1,)]
    return pl.pallas_call(
        functools.partial(reduce_kernel, count),
        out_shape=(
            jax.ShapeDtypeStruct((rows, in_dim), jnp.float32),
            jax.ShapeDtypeStruct((in_dim, GROUP * cut), jnp.float32),
            jax.ShapeDtypeStruct((1, GROUP * cut), jnp.float32),
        ),
        in_specs=[VMEM, VMEM],
        out_specs=(VMEM, VMEM, VMEM),
        scratch_shapes=[
            pltpu.VMEM((SIDES, 2) + piece, jnp.bfloat16),
            pltpu.VMEM((SIDES,) + piece, jnp.bfloat16),
            pltpu.VMEM((SIDES,) + piece, jnp.bfloat16),
            pltpu.VMEM((2,) + piece, jnp.bfloat16),
            pltpu.VMEM((2,) + piece, jnp.bfloat16),
            pltpu.VMEM((GROUP - 1, blocks, share, cut), jnp.float32),
            pltpu.VMEM((blocks - 1, share, cut), jnp.float32),
            pltpu.VMEM((blocks, share, cut), jnp.float32),
            pltpu.VMEM((GROUP, blocks, share, cut), jnp.float32),
        ] + [dma(shape) for shape in pairs for _ in range(2)],
        compiler_params=pltpu.CompilerParams(
            collective_id=1, has_side_effects=True, vmem_limit_bytes=LIMIT),
        name="reduce_terms",
    )(terms, grads)


def on_device(features, weight, bias, tile_values, tile_cols, tile_counts, out_grad):
    rows = features.shape[0]
    blocks = lax.axis_size("blk")
    nodes = rows * lax.axis_size("rep") * blocks
    window = gather(features)
    activations, terms, grads = layer(
        tile_counts, tile_cols, window, tile_values, weight, bias, out_grad,
        1.0 / math.sqrt(nodes), blocks)
    feature_grad, weight_grad, bias_grad = reduce(terms, grads, rows)
    return activations, feature_grad, weight_grad, bias_grad.reshape(-1)


def solution(mesh):
    assert mesh.shape["rep"] == GROUP
    rows = P(("blk", "rep"), None)
    return jax.shard_map(
        on_device, mesh=mesh,
        in_specs=(rows, P(), P(), rows, rows, P(("blk", "rep")), rows),
        out_specs=(rows, rows, P(), P()), check_vma=False,
    )
```

time: 379 us -> 92.7 us (0.24)
  waiting for transfers between devices: 167 us -> 0 us
  other arithmetic: 90.8 us -> 0 us
  Pallas kernels: 0 us -> 85.8 us
  blocking collectives: 39.4 us -> 0 us
  local copies, waits for them, and re-layouts: 38.1 us -> 4.8 us
  matrix products: 18.1 us -> 0 us
  between operations: 13.9 us -> 0.65 us
  starting transfers between devices: 10.3 us -> 0 us
    pallas_call x0 -> x3, Pallas kernels: none -> 85.8 us  [the longest x1 35.3 us: reduce(): pl.pallas_call(functools.partial(reduce_kernel, count), out_shape=(jax.Sh...]
    psum x1 -> x0, waiting for transfers between devices: 54.8 us -> none  [on_device(): lax.psum((local_weight, local_bias), ('blk', 'rep'))]
    scatter-add x1 -> x0, other arithmetic: 52.6 us -> none  [on_device(): placed = jnp.zeros((window_count, TILE, in_dim), jnp.float32).at[tile_col...]
    ppermute x4 -> x0, waiting for transfers between devices: 52.1 us -> none  [passed_along(): return lax.ppermute(value, axis, pairs)]
    psum x1 -> x0, blocking collectives: 39.4 us -> none  [on_device(): lax.psum((local_weight, local_bias), ('blk', 'rep'))]
    reduce_scatter x1 -> x0, waiting for transfers between devices: 33.6 us -> none  [on_device(): lax.psum_scatter(block_total, 'rep', scatter_dimension=0, tiled=True)]
    select_n x4 -> x0, other arithmetic: 28.6 us -> none  [the longest x1 16.3 us: on_device(): jnp.where(is_live[:, :, None, None], gathered, jnp.zeros((), gathered.dty...]
    all_gather x1 -> x0, waiting for transfers between devices: 26.1 us -> none  [on_device(): lax.all_gather(stacked, 'rep', axis=1, tiled=True).reshape(-1, in_dim)]
  transfers between devices with their start and end apart: 7 -> 0, of which waited for: 6 -> 0; matrix products, arithmetic and copies ran while one was open for 2% -> 0% of each run, Pallas kernels for 0% -> 0%
where the time goes in v1:
time: 92.7 us; the launch traced here: 91.3 us
  Pallas kernels  85.8 us (93%)
  local copies, waits for them, and re-layouts  4.8 us (5%)
    pallas_call x1, Pallas kernels, reduce(): pl.pallas_call(functools.partial(reduce_kernel, count), out_shape=(jax.Sh...  35.3 us
    pallas_call x1, Pallas kernels, gather(): pl.pallas_call(functools.partial(gather_kernel, lax.axis_size('blk')), ou...  29.1 us
    pallas_call x1, Pallas kernels, layer(): pl.pallas_call(functools.partial(layer_kernel, factor), out_shape=(jax.Sh...  21.4 us
    unnamed x3, local copies, waits for them, and re-layouts  4.8 us

profile of v1, /device:TPU:0, one launch (start us, length us, event | category | flops | bytes accessed | tf_op | source)
XLA Modules:
  0.0 91.3 jit_solution(12341157088931690908)
XLA Ops:
  0.6 29.1 %gather_window.1 = bf16[3,4,1024,128]{3,2,1,0:T(8,128)(2,1)} custom-call(bf16[1024,128]{1,0:T(8,128)(2,1)} %own_ref.1), custom_call_target="tpu_custom_call" | custom-call | tf_op jit(solution)/shard_map/gather_window/pallas_call | solution.py:104
  29.7 21.4 %layer.1 = (bf16[1024,512]{1,0:T(8,128)(2,1)}, bf16[96,128,128]{2,1,0:T(8,128)(2,1)}, f32[4,8,24,128]{3,2,1,0:T(8,128)}) custom-call(s32[8]{0:T(128)} %counts.1, s32[8,32]{1,0:T(8,128)} %cols.1, bf16[96,128,128]{2,1,0:T(8,128)(2,1)} %bitcast.4, bf16[1024,4096]{1,0:T(8,128)(2,1)} %val_hbm.1, bf16[128,512]{1,0:T(8,128)(2,1)} %weight.1, f32[1,512]{1,0:T(1,128)} %bitcast.6, ...), custom_call_target="tpu_custom_call" | custom-call | tf_op jit(solution)/shard_map/layer/pallas_call | solution.py:237
  51.1 35.3 %reduce_terms.1 = (f32[1024,128]{1,0:T(8,128)}, f32[128,512]{1,0:T(8,128)}, f32[1,512]{1,0:T(1,128)}) custom-call(bf16[3,4,8,128,128]{4,3,2,1,0:T(8,128)(2,1)} %bitcast.5, f32[4,8,24,128]{3,2,1,0:T(8,128)} %get-tuple-element.12.grads), custom_call_target="tpu_custom_call" | custom-call | tf_op jit(solution)/shard_map/reduce_terms/pallas_call | solution.py:394
  86.5 1.9 %copy.14 = f32[1024,128]{1,0:T(8,128)} copy(f32[1024,128]{1,0:T(8,128)} %get-tuple-element.21) | data formatting | bytes 1048576
  88.3 1.7 %copy.15 = f32[128,512]{1,0:T(8,128)} copy(f32[128,512]{1,0:T(8,128)} %get-tuple-element.22) | data formatting | bytes 524288
  90.0 1.3 %copy.16 = f32[512]{0:T(512)} copy(f32[512]{0:T(512)} %bitcast.7) | data formatting | bytes 4096

commit v2 on v1

v2 whole, which is shorter than its diff:
```python
import functools
import math

import jax
import jax.numpy as jnp
from jax import lax
from jax.experimental import pallas as pl
from jax.experimental.pallas import tpu as pltpu
from jax.sharding import PartitionSpec as P

TILE = 128
SIDES = 3
GROUP = 4
CHUNKS = 4
SPAN = 8
BIAS_ROWS = 16
SUM_ROWS = 8
MESH = pl.DeviceIdType.MESH
VMEM = pl.BlockSpec(memory_space=pltpu.VMEM)
SMEM = pl.BlockSpec(memory_space=pltpu.SMEM)
ANY = pl.BlockSpec(memory_space=pl.ANY)
LIMIT = 56 * 1024 * 1024


def partners():
    rep = lax.axis_index("rep")
    return rep + 1 - 2 * (rep % 2), (rep + 2) % GROUP


def gather_kernel(count, own_ref, win_ref, own_sem, blk_send, blk_recv, far_send, far_recv,
                  near_send, near_recv, turn_send, turn_recv):
    blk, rep = lax.axis_index("blk"), lax.axis_index("rep")
    near, far = partners()
    before, after = (blk + count - 1) % count, (blk + 1) % count
    rows = own_ref.shape[0] // CHUNKS
    turned = CHUNKS - 1
    plain = range(CHUNKS - 1)

    barrier = pltpu.get_barrier_semaphore()
    for device in ((before, rep), (after, rep), (blk, near), (blk, far)):
        pl.semaphore_signal(barrier, inc=1, device_id=device, device_id_type=MESH)
    pl.semaphore_wait(barrier, 4)

    started = []

    def start(side, member, chunk, send, recv, device, own=False, lands=None):
        here = pl.ds(chunk * rows, rows)
        source = own_ref.at[here] if own else win_ref.at[side, member, here]
        target = win_ref.at[side if lands is None else lands, member, here]
        copy = pltpu.make_async_remote_copy(
            src_ref=source, dst_ref=target, send_sem=send, recv_sem=recv,
            device_id=device, device_id_type=MESH)
        copy.start()
        started.append(copy)
        return copy

    ways = ((0, after), (2, before))

    def to_blk(which, chunk):
        lands, target = ways[which]
        return start(1, rep, chunk, blk_send.at[which, chunk], blk_recv.at[which, chunk],
                     (target, rep), own=True, lands=lands)

    def to_turn(which):
        lands, target = ways[which]
        return start(1, far, turned, turn_send.at[which], turn_recv.at[which], (target, rep),
                     lands=lands)

    def to_far(side, chunk):
        return start(side, rep, chunk, far_send.at[side, chunk], far_recv.at[side, chunk],
                     (blk, far), own=side == 1)

    near_copies = []

    def to_near(side, whose, chunk):
        near_copies.append(start(
            side, (rep, far)[whose], chunk, near_send.at[side, whose, chunk],
            near_recv.at[side, whose, chunk], (blk, near), own=side == 1 and whose == 0))

    blk_copies, far_copies = {}, {}
    far_copies[1, turned] = to_far(1, turned)
    for chunk in range(CHUNKS):
        for which in range(2):
            blk_copies[which, chunk] = to_blk(which, chunk)
        if chunk in plain:
            far_copies[1, chunk] = to_far(1, chunk)
    for chunk in range(CHUNKS):
        to_near(1, 0, chunk)
    local = pltpu.make_async_copy(own_ref, win_ref.at[1, rep], own_sem)
    local.start()

    far_copies[1, turned].wait_recv()
    turns = [to_turn(which) for which in range(2)]
    to_near(1, 1, turned)
    for chunk in range(CHUNKS):
        for which in range(2):
            side = ways[which][0]
            blk_copies[which, chunk].wait_recv()
            if chunk in plain:
                far_copies[side, chunk] = to_far(side, chunk)
            to_near(side, 0, chunk)
    for chunk in plain:
        far_copies[1, chunk].wait_recv()
        to_near(1, 1, chunk)
    for which in range(2):
        turns[which].wait_recv()
        to_near(ways[which][0], 1, turned)
    for chunk in plain:
        for side in (0, 2):
            far_copies[side, chunk].wait_recv()
            to_near(side, 1, chunk)
    for copy in near_copies:
        copy.wait_recv()
    for copy in started:
        copy.wait_send()
    local.wait()


def gather(features):
    rows, width = features.shape
    dma = pltpu.SemaphoreType.DMA
    return pl.pallas_call(
        functools.partial(gather_kernel, lax.axis_size("blk")),
        out_shape=jax.ShapeDtypeStruct((SIDES, GROUP, rows, width), features.dtype),
        in_specs=[VMEM],
        out_specs=VMEM,
        scratch_shapes=[
            dma, dma((2, CHUNKS)), dma((2, CHUNKS)), dma((SIDES, CHUNKS)), dma((SIDES, CHUNKS)),
            dma((SIDES, 2, CHUNKS)), dma((SIDES, 2, CHUNKS)), dma((2,)), dma((2,)),
        ],
        compiler_params=pltpu.CompilerParams(
            collective_id=0, has_side_effects=True, vmem_limit_bytes=LIMIT),
        name="gather_window",
    )(features)


def gelu_parts(pre_act):
    inner = 0.7978845608028654 * (pre_act + 0.044715 * pre_act * pre_act * pre_act)
    tangent = jnp.tanh(inner)
    half = 0.5 * (1.0 + tangent)
    value_part = pre_act * half
    slope = half + 0.5 * pre_act * (
        1.0 - tangent * tangent
    ) * 0.7978845608028654 * (1.0 + 0.134145 * pre_act * pre_act)
    return value_part, slope


def layer_kernel(factor, counts, cols, win_hbm, val_hbm, weight, bias, og_hbm, act_out, terms_out,
                 grad_out, vals, win, og, placed, agg, pre_grad, row_grad, acc, bias_sum, val_sem,
                 win_sem, og_sem):
    tiles, _, wide = vals.shape
    spans = wide // (SPAN * TILE)
    win_copy = pltpu.make_async_copy(win_hbm, win, win_sem)
    og_copy = pltpu.make_async_copy(og_hbm, og, og_sem)

    def val_copy(t):
        return pltpu.make_async_copy(val_hbm.at[pl.ds(t * TILE, TILE)], vals.at[t], val_sem.at[t])

    win_copy.start()
    for t in range(tiles):
        val_copy(t).start()
    og_copy.start()

    def clear(w, carry):
        placed[w] = jnp.zeros(placed.shape[1:], placed.dtype)
        return carry

    lax.fori_loop(0, placed.shape[0], clear, 0)
    win_copy.wait()

    def forward(t, carry):
        val_copy(t).wait()
        live = counts[t]
        acc[...] = jnp.zeros_like(acc)
        for span in range(spans):

            @pl.when(span * SPAN < live)
            def _():
                picked = []
                for k in range(SPAN):
                    tile = win[cols[t, span * SPAN + k]]
                    picked.append(jnp.where(span * SPAN + k < live, tile, jnp.zeros_like(tile)))
                acc[...] += jnp.dot(
                    vals[t, :, span * SPAN * TILE:(span + 1) * SPAN * TILE],
                    jnp.concatenate(picked, axis=0), preferred_element_type=jnp.float32)

        agg[pl.ds(pl.multiple_of(t * TILE, TILE), TILE)] = acc[...].astype(agg.dtype)
        return carry

    lax.fori_loop(0, tiles, forward, 0)
    og_copy.wait()
    bias_sum[...] = jnp.zeros_like(bias_sum)

    def dense(t, carry):
        here = pl.ds(pl.multiple_of(t * TILE, TILE), TILE)
        pre_act = jnp.dot(agg[here], weight[...], preferred_element_type=jnp.float32) + bias[...]
        value_part, slope = gelu_parts(pre_act)
        act_out[here] = value_part.astype(act_out.dtype)
        grad = (og[here].astype(jnp.float32) * slope).astype(jnp.bfloat16)
        pre_grad[here] = grad
        bias_sum[...] += jnp.sum(
            grad.astype(jnp.float32).reshape(TILE // 8, 8, grad.shape[1]), axis=0)
        row_grad[t] = lax.dot_general(
            weight[...], grad, (((1,), (1,)), ((), ())), preferred_element_type=jnp.float32
        ).astype(row_grad.dtype)
        return carry

    lax.fori_loop(0, tiles, dense, 0)
    weight_grad = lax.dot_general(
        agg[...], pre_grad[...], (((0,), (0,)), ((), ())), preferred_element_type=jnp.float32
    ) * factor
    bias_grad = jnp.sum(bias_sum[...], axis=0, keepdims=True) * factor
    members, _, cut = grad_out.shape
    in_dim = agg.shape[1]
    for member in range(members):
        columns = slice(member * cut, (member + 1) * cut)
        grad_out[member, :in_dim] = weight_grad[:, columns].astype(grad_out.dtype)
        grad_out[member, in_dim:] = jnp.broadcast_to(
            bias_grad[:, columns], (BIAS_ROWS, cut)).astype(grad_out.dtype)

    def backward(t, carry):
        live = counts[t]
        for span in range(spans):

            @pl.when(span * SPAN < live)
            def _():
                terms = jnp.dot(
                    row_grad[t], vals[t, :, span * SPAN * TILE:(span + 1) * SPAN * TILE],
                    preferred_element_type=jnp.float32)
                for k in range(SPAN):
                    term = terms[:, k * TILE:(k + 1) * TILE]
                    term = jnp.where(span * SPAN + k < live, term, jnp.zeros_like(term))
                    placed[cols[t, span * SPAN + k]] += term

        return carry

    lax.fori_loop(0, tiles, backward, 0)

    def hand_on(w, carry):
        terms_out[w] = placed[w].astype(terms_out.dtype)
        return carry

    lax.fori_loop(0, placed.shape[0], hand_on, 0)


def layer(counts, cols, window, values, weight, bias, out_grad, factor):
    rows, wide = values.shape
    in_dim, out_dim = weight.shape
    tiles = rows // TILE
    window_tiles = SIDES * GROUP * tiles
    dma = pltpu.SemaphoreType.DMA
    window_shape = (window_tiles, TILE, in_dim)
    grad_shape = (GROUP, in_dim + BIAS_ROWS, out_dim // GROUP)
    return pl.pallas_call(
        functools.partial(layer_kernel, factor),
        out_shape=(
            jax.ShapeDtypeStruct((rows, out_dim), jnp.bfloat16),
            jax.ShapeDtypeStruct((window_tiles, in_dim, TILE), jnp.bfloat16),
            jax.ShapeDtypeStruct(grad_shape, jnp.bfloat16),
        ),
        in_specs=[SMEM, SMEM, ANY, ANY, VMEM, VMEM, ANY],
        out_specs=(VMEM, VMEM, VMEM),
        scratch_shapes=[
            pltpu.VMEM((tiles, TILE, wide), jnp.bfloat16),
            pltpu.VMEM(window_shape, jnp.bfloat16),
            pltpu.VMEM((rows, out_dim), jnp.bfloat16),
            pltpu.VMEM((window_tiles, in_dim, TILE), jnp.float32),
            pltpu.VMEM((rows, in_dim), jnp.bfloat16),
            pltpu.VMEM((rows, out_dim), jnp.bfloat16),
            pltpu.VMEM((tiles, in_dim, TILE), jnp.bfloat16),
            pltpu.VMEM((TILE, in_dim), jnp.float32),
            pltpu.VMEM((8, out_dim), jnp.float32),
            dma((tiles,)), dma, dma,
        ],
        compiler_params=pltpu.CompilerParams(vmem_limit_bytes=LIMIT),
        name="layer",
    )(counts, cols, window.reshape(window_shape), values, weight, bias.reshape(1, -1), out_grad)


def reduce_kernel(count, terms, grads, out_ref, whole, near_buf, far_out, far_buf, blk_out,
                  blk_buf, turn_buf, rep_buf, share_out, share_buf, summed, near_send, near_recv,
                  far_send, far_recv, blk_send, blk_recv, turn_send, turn_recv, rep_send, rep_recv,
                  share_send, share_recv, back_send, back_recv, last_send, last_recv):
    blk, rep = lax.axis_index("blk"), lax.axis_index("rep")
    near, far = partners()
    across = (near + 2) % GROUP
    before, after = (blk + count - 1) % count, (blk + 1) % count
    step = out_ref.shape[0] // CHUNKS
    turned = CHUNKS - 1
    plain = range(CHUNKS - 1)
    f32 = jnp.float32

    barrier = pltpu.get_barrier_semaphore()
    for turn in range(1, GROUP):
        pl.semaphore_signal(
            barrier, inc=1, device_id=(blk, (rep + turn) % GROUP), device_id_type=MESH)
    for turn in range(1, count):
        pl.semaphore_signal(
            barrier, inc=1, device_id=((blk + turn) % count, rep), device_id_type=MESH)
    pl.semaphore_wait(barrier, GROUP + count - 2)

    started = []

    def start(source, target, send, recv, device):
        copy = pltpu.make_async_remote_copy(
            src_ref=source, dst_ref=target, send_sem=send, recv_sem=recv,
            device_id=device, device_id_type=MESH)
        copy.start()
        started.append(copy)
        return copy

    def to_reps(source, target, send, recv):
        return [
            start(source(turn), target(turn), send.at[turn - 1], recv.at[turn - 1],
                  (blk, (rep + turn) % GROUP))
            for turn in range(1, GROUP)
        ]

    def to_blks(source, target, send, recv):
        return [
            start(source(turn), target(turn), send.at[turn - 1], recv.at[turn - 1],
                  ((blk + turn) % count, rep))
            for turn in range(1, count)
        ]

    near_copies, far_copies, blk_copies, turn_copies = {}, {}, {}, {}
    ways = ((0, before), (2, after))

    def to_near(side, whose):
        near_copies[side, whose] = start(
            terms.at[side, (near, across)[whose]], near_buf.at[side, whose],
            near_send.at[side, whose], near_recv.at[side, whose], (blk, near))

    to_near(0, 1)
    to_near(2, 1)
    rep_copies = to_reps(
        lambda turn: grads.at[(rep + turn) % GROUP], lambda turn: rep_buf.at[turn - 1],
        rep_send, rep_recv)
    for side, whose in ((0, 0), (2, 0), (1, 1), (1, 0)):
        to_near(side, whose)

    def here(chunk):
        return pl.ds(chunk * step, step)

    def chip_sum(side, whose, chunk):
        part = here(chunk)
        return (terms[side, (rep, far)[whose], part].astype(f32)
                + near_buf[side, whose, part].astype(f32))

    def to_far(side, chunk, value):
        part = here(chunk)
        far_out[side, part] = value.astype(far_out.dtype)
        far_copies[side, chunk] = start(
            far_out.at[side, part], far_buf.at[side, part], far_send.at[side, chunk],
            far_recv.at[side, chunk], (blk, far))

    def to_blk(which, chunk, value):
        part = here(chunk)
        blk_out[which, part] = value.astype(blk_out.dtype)
        blk_copies[which, chunk] = start(
            blk_out.at[which, part], blk_buf.at[which, part], blk_send.at[which, chunk],
            blk_recv.at[which, chunk], (ways[which][1], rep))

    near_copies[0, 1].wait_recv()
    near_copies[2, 1].wait_recv()
    for which, (side, block) in enumerate(ways):
        part = here(turned)
        far_out[side, part] = chip_sum(side, 1, turned).astype(far_out.dtype)
        turn_copies[which] = start(
            far_out.at[side, part], turn_buf.at[which], turn_send.at[which], turn_recv.at[which],
            (block, rep))
    for chunk in plain:
        for side in (0, 2):
            to_far(side, chunk, chip_sum(side, 1, chunk))

    for copy in rep_copies:
        copy.wait_recv()
    in_dim = grads.shape[1] - BIAS_ROWS
    share = in_dim // count
    total = grads[rep].astype(f32)
    for turn in range(1, GROUP):
        total += rep_buf[turn - 1].astype(f32)
    share_out[:, :share] = total[:in_dim].reshape(count, share, total.shape[1])
    share_out[:, share:] = jnp.broadcast_to(
        total[in_dim:in_dim + SUM_ROWS][None], (count, SUM_ROWS, total.shape[1]))
    share_copies = to_blks(
        lambda turn: share_out.at[(blk + turn) % count], lambda turn: share_buf.at[turn - 1],
        share_send, share_recv)

    near_copies[0, 0].wait_recv()
    near_copies[2, 0].wait_recv()
    for which, (side, _) in enumerate(ways):
        to_blk(which, turned, chip_sum(side, 0, turned))
    near_copies[1, 1].wait_recv()
    for chunk in plain:
        to_far(1, chunk, chip_sum(1, 1, chunk))
    own = chip_sum(1, 1, turned)
    for which in range(2):
        turn_copies[which].wait_recv()
        own += turn_buf[which].astype(f32)
    to_far(1, turned, own)

    for chunk in plain:
        for which, (side, _) in enumerate(ways):
            far_copies[side, chunk].wait_recv()
            to_blk(which, chunk,
                   chip_sum(side, 0, chunk) + far_buf[side, here(chunk)].astype(f32))
        if chunk == 0:
            for copy in share_copies:
                copy.wait_recv()
            mine = share_out[blk]
            for turn in range(1, count):
                mine += share_buf[turn - 1]
            summed[blk] = mine
            back_copies = to_blks(
                lambda turn: summed.at[blk], lambda turn: summed.at[blk], back_send, back_recv)

    for copy in back_copies:
        copy.wait_recv()
    whole[rep, :in_dim] = summed[:, :share].reshape(in_dim, total.shape[1]).astype(whole.dtype)
    whole[rep, in_dim:] = jnp.broadcast_to(
        summed[0, share:share + 1], (BIAS_ROWS, total.shape[1])).astype(whole.dtype)
    last_copies = to_reps(
        lambda turn: whole.at[rep], lambda turn: whole.at[rep], last_send, last_recv)

    near_copies[1, 0].wait_recv()
    for chunk in (turned, *plain):
        part = here(chunk)
        for which in range(2):
            blk_copies[which, chunk].wait_recv()
        far_copies[1, chunk].wait_recv()
        total = chip_sum(1, 0, chunk) + far_buf[1, part].astype(f32)
        for which in range(2):
            total += blk_buf[which, part].astype(f32)
        out_ref[part] = total

    for copy in last_copies:
        copy.wait_recv()
    for copy in started:
        copy.wait_send()


def reduce(terms, grads):
    count = lax.axis_size("blk")
    tiles, in_dim, _ = terms.shape
    tiles = tiles // (SIDES * GROUP)
    terms = terms.reshape(SIDES, GROUP, tiles, in_dim, TILE)
    cut = grads.shape[2]
    share = in_dim // count + SUM_ROWS
    piece = (tiles, in_dim, TILE)
    dma = pltpu.SemaphoreType.DMA
    pairs = [(SIDES, 2), (SIDES, CHUNKS), (2, CHUNKS), (2,), (GROUP - 1,), (count - 1,),
             (count - 1,), (GROUP - 1,)]
    return pl.pallas_call(
        functools.partial(reduce_kernel, count),
        out_shape=(
            jax.ShapeDtypeStruct(piece, jnp.float32),
            jax.ShapeDtypeStruct(grads.shape, jnp.bfloat16),
        ),
        in_specs=[VMEM, VMEM],
        out_specs=(VMEM, VMEM),
        scratch_shapes=[
            pltpu.VMEM((SIDES, 2) + piece, jnp.bfloat16),
            pltpu.VMEM((SIDES,) + piece, jnp.bfloat16),
            pltpu.VMEM((SIDES,) + piece, jnp.bfloat16),
            pltpu.VMEM((2,) + piece, jnp.bfloat16),
            pltpu.VMEM((2,) + piece, jnp.bfloat16),
            pltpu.VMEM((2, tiles // CHUNKS) + piece[1:], jnp.bfloat16),
            pltpu.VMEM((GROUP - 1,) + grads.shape[1:], jnp.bfloat16),
            pltpu.VMEM((count, share, cut), jnp.float32),
            pltpu.VMEM((count - 1, share, cut), jnp.float32),
            pltpu.VMEM((count, share, cut), jnp.float32),
        ] + [dma(shape) for shape in pairs for _ in range(2)],
        compiler_params=pltpu.CompilerParams(
            collective_id=1, has_side_effects=True, vmem_limit_bytes=LIMIT),
        name="reduce_terms",
    )(terms, grads)


def finish_kernel(turned, whole, feature_out, weight_out, bias_out):
    in_dim, cut = weight_out.shape[0], whole.shape[2]
    for tile in range(turned.shape[0]):
        feature_out[tile * TILE:(tile + 1) * TILE] = turned[tile].T
    for member in range(GROUP):
        columns = slice(member * cut, (member + 1) * cut)
        weight_out[:, columns] = whole[member, :in_dim].astype(jnp.float32)
        bias_out[:, columns] = whole[member, in_dim:].astype(jnp.float32)[:1]


def finish(turned, whole):
    tiles, in_dim, _ = turned.shape
    out_dim = GROUP * whole.shape[2]
    return pl.pallas_call(
        finish_kernel,
        out_shape=(
            jax.ShapeDtypeStruct((tiles * TILE, in_dim), jnp.float32),
            jax.ShapeDtypeStruct((in_dim, out_dim), jnp.float32),
            jax.ShapeDtypeStruct((1, out_dim), jnp.float32),
        ),
        in_specs=[VMEM, VMEM],
        out_specs=(VMEM, VMEM, VMEM),
        compiler_params=pltpu.CompilerParams(vmem_limit_bytes=LIMIT),
        name="finish",
    )(turned, whole)


def on_device(features, weight, bias, tile_values, tile_cols, tile_counts, out_grad):
    nodes = features.shape[0] * lax.axis_size("rep") * lax.axis_size("blk")
    window = gather(features)
    activations, terms, grads = layer(
        tile_counts, tile_cols, window, tile_values, weight, bias, out_grad,
        1.0 / math.sqrt(nodes))
    feature_grad, weight_grad, bias_grad = finish(*reduce(terms, grads))
    return activations, feature_grad, weight_grad, bias_grad.reshape(-1)


def solution(mesh):
    assert mesh.shape["rep"] == GROUP
    rows = P(("blk", "rep"), None)
    return jax.shard_map(
        on_device, mesh=mesh,
        in_specs=(rows, P(), P(), rows, rows, P(("blk", "rep")), rows),
        out_specs=(rows, rows, P(), P()), check_vma=False,
    )
```

time: 92.7 us -> 80.5 us (0.87); the launches traced: 91.3 us -> 80 us
  Pallas kernels: 85.8 us -> 79.4 us
  local copies, waits for them, and re-layouts: 4.8 us -> 0 us
    pallas_call x1, Pallas kernels: 35.3 us -> 26.4 us  [reduce(): pl.pallas_call(functools.partial(reduce_kernel, count), out_shape=(jax.Sh...]
    unnamed x3 -> x0, local copies, waits for them, and re-layouts: 4.8 us -> none
    pallas_call x1, Pallas kernels: 21.4 us -> 24.5 us  [layer(): pl.pallas_call(functools.partial(layer_kernel, factor), out_shape=(jax.Sh...]
    pallas_call x1, Pallas kernels: 29.1 us -> 26.3 us  [gather(): pl.pallas_call(functools.partial(gather_kernel, lax.axis_size('blk')), ou...]
    pallas_call x0 -> x1, Pallas kernels: none -> 2.09 us  [finish(): pl.pallas_call(finish_kernel, out_shape=(jax.ShapeDtypeStruct((tiles * TI...]
where the time goes in v2:
time: 80.5 us; the launch traced here: 80 us
  Pallas kernels  79.4 us (99%)
    pallas_call x1, Pallas kernels, reduce(): pl.pallas_call(functools.partial(reduce_kernel, count), out_shape=(jax.Sh...  26.4 us
    pallas_call x1, Pallas kernels, gather(): pl.pallas_call(functools.partial(gather_kernel, lax.axis_size('blk')), ou...  26.3 us
    pallas_call x1, Pallas kernels, layer(): pl.pallas_call(functools.partial(layer_kernel, factor), out_shape=(jax.Sh...  24.5 us
    pallas_call x1, Pallas kernels, finish(): pl.pallas_call(finish_kernel, out_shape=(jax.ShapeDtypeStruct((tiles * TI...  2.09 us

profile of v2, /device:TPU:0, one launch (start us, length us, event | category | flops | bytes accessed | tf_op | source)
XLA Modules:
  0.0 80.0 jit_solution(13274644878129553566)
XLA Ops:
  0.6 26.3 %gather_window.1 = bf16[3,4,1024,128]{3,2,1,0:T(8,128)(2,1)} custom-call(bf16[1024,128]{1,0:T(8,128)(2,1)} %own_ref.1), custom_call_target="tpu_custom_call" | custom-call | tf_op jit(solution)/shard_map/gather_window/pallas_call | solution.py:122
  27.0 24.5 %layer.1 = (bf16[1024,512]{1,0:T(8,128)(2,1)}, bf16[96,128,128]{2,1,0:T(8,128)(2,1)}, bf16[4,144,128]{2,1,0:T(8,128)(2,1)}) custom-call(s32[8]{0:T(128)} %counts.1, s32[8,32]{1,0:T(8,128)} %cols.1, bf16[96,128,128]{2,1,0:T(8,128)(2,1)} %bitcast.4, bf16[1024,4096]{1,0:T(8,128)(2,1)} %val_hbm.1, bf16[128,512]{1,0:T(8,128)(2,1)} %weight.1, f32[1,512]{1,0:T(1,128)} %bitcast.6, ...), custom_call_target="tpu_custom_call" | custom-call | tf_op jit(solution)/shard_map/layer/pallas_call | solution.py:254
  51.5 26.4 %reduce_terms.1 = (f32[8,128,128]{2,1,0:T(8,128)}, bf16[4,144,128]{2,1,0:T(8,128)(2,1)}) custom-call(bf16[3,4,8,128,128]{4,3,2,1,0:T(8,128)(2,1)} %bitcast.5, bf16[4,144,128]{2,1,0:T(8,128)(2,1)} %get-tuple-element.14.grads), custom_call_target="tpu_custom_call" | custom-call | tf_op jit(solution)/shard_map/reduce_terms/pallas_call | solution.py:454
  77.9 2.1 %finish.1 = (f32[1024,128]{1,0:T(8,128)}, f32[128,512]{1,0:T(8,128)}, f32[1,512]{1,0:T(1,128)}) custom-call(f32[8,128,128]{2,1,0:T(8,128)} %get-tuple-element.15.turned, bf16[4,144,128]{2,1,0:T(8,128)(2,1)} %get-tuple-element.16.whole), custom_call_target="tpu_custom_call" | custom-call | tf_op jit(solution)/shard_map/finish/pallas_call | solution.py:493

commit v3 on v2

--- a/solution.py
+++ b/solution.py
@@ -12,6 +12,8 @@
 SIDES = 3
 GROUP = 4
 CHUNKS = 4
+PLAIN = (0, 1)
+TURNED = (2, 3)
 SPAN = 8
 BIAS_ROWS = 16
 SUM_ROWS = 8
@@ -27,88 +29,108 @@
     return rep + 1 - 2 * (rep % 2), (rep + 2) % GROUP
 
 
-def gather_kernel(count, own_ref, win_ref, own_sem, blk_send, blk_recv, far_send, far_recv,
-                  near_send, near_recv, turn_send, turn_recv):
+def lines(count):
+    blk = lax.axis_index("blk")
+    odd = blk % 2
+    pair = blk + 1 - 2 * odd
+    onward = (blk + 2 - 4 * odd + count) % count
+    behind = (blk + 4 * odd - 2 + count) % count
+    return pair, onward, behind, 2 * odd, 2 - 2 * odd
+
+
+def gather_kernel(count, own_ref, win_ref, own_sem, pair_send, pair_recv, on_send, on_recv,
+                  far_send, far_recv, near_send, near_recv):
     blk, rep = lax.axis_index("blk"), lax.axis_index("rep")
     near, far = partners()
-    before, after = (blk + count - 1) % count, (blk + 1) % count
+    pair, onward, behind, on_side, pair_side = lines(count)
+    sides = (on_side, 1, pair_side)
     rows = own_ref.shape[0] // CHUNKS
-    turned = CHUNKS - 1
-    plain = range(CHUNKS - 1)
 
     barrier = pltpu.get_barrier_semaphore()
-    for device in ((before, rep), (after, rep), (blk, near), (blk, far)):
+    for device in ((pair, rep), (onward, rep), (behind, rep), (blk, near), (blk, far)):
         pl.semaphore_signal(barrier, inc=1, device_id=device, device_id_type=MESH)
-    pl.semaphore_wait(barrier, 4)
+    pl.semaphore_wait(barrier, 5)
 
     started = []
 
-    def start(side, member, chunk, send, recv, device, own=False, lands=None):
+    def start(side, member, chunk, lands, send, recv, device):
         here = pl.ds(chunk * rows, rows)
-        source = own_ref.at[here] if own else win_ref.at[side, member, here]
-        target = win_ref.at[side if lands is None else lands, member, here]
+        source = win_ref.at[sides[side], (rep, far)[member], here]
+        if side == 1 and member == 0:
+            source = own_ref.at[here]
         copy = pltpu.make_async_remote_copy(
-            src_ref=source, dst_ref=target, send_sem=send, recv_sem=recv,
-            device_id=device, device_id_type=MESH)
+            src_ref=source, dst_ref=win_ref.at[sides[lands], (rep, far)[member], here],
+            send_sem=send, recv_sem=recv, device_id=device, device_id_type=MESH)
         copy.start()
         started.append(copy)
         return copy
 
-    ways = ((0, after), (2, before))
-
-    def to_blk(which, chunk):
-        lands, target = ways[which]
-        return start(1, rep, chunk, blk_send.at[which, chunk], blk_recv.at[which, chunk],
-                     (target, rep), own=True, lands=lands)
-
-    def to_turn(which):
-        lands, target = ways[which]
-        return start(1, far, turned, turn_send.at[which], turn_recv.at[which], (target, rep),
-                     lands=lands)
+    pair_copies, on_copies, far_copies, near_copies = {}, {}, {}, []
+
+    def to_pair(member, chunk):
+        pair_copies[member, chunk] = start(
+            1, member, chunk, 0, pair_send.at[member, chunk], pair_recv.at[member, chunk],
+            (pair, rep))
+
+    def to_onward(member, chunk):
+        on_copies[member, chunk] = start(
+            2, member, chunk, 0, on_send.at[member, chunk], on_recv.at[member, chunk],
+            (onward, rep))
 
     def to_far(side, chunk):
-        return start(side, rep, chunk, far_send.at[side, chunk], far_recv.at[side, chunk],
-                     (blk, far), own=side == 1)
-
-    near_copies = []
-
-    def to_near(side, whose, chunk):
+        far_copies[side, chunk] = start(
+            side, 0, chunk, side, far_send.at[side, chunk], far_recv.at[side, chunk], (blk, far))
+
+    def to_near(side, member, chunk):
         near_copies.append(start(
-            side, (rep, far)[whose], chunk, near_send.at[side, whose, chunk],
-            near_recv.at[side, whose, chunk], (blk, near), own=side == 1 and whose == 0))
-
-    blk_copies, far_copies = {}, {}
-    far_copies[1, turned] = to_far(1, turned)
-    for chunk in range(CHUNKS):
-        for which in range(2):
-            blk_copies[which, chunk] = to_blk(which, chunk)
-        if chunk in plain:
-            far_copies[1, chunk] = to_far(1, chunk)
-    for chunk in range(CHUNKS):
+            side, member, chunk, side, near_send.at[side, member, chunk],
+            near_recv.at[side, member, chunk], (blk, near)))
+
+    order = PLAIN + TURNED
+    for own, over in zip(order, TURNED + PLAIN):
+        to_pair(0, own)
+        to_far(1, over)
+    for chunk in order:
         to_near(1, 0, chunk)
     local = pltpu.make_async_copy(own_ref, win_ref.at[1, rep], own_sem)
     local.start()
 
-    far_copies[1, turned].wait_recv()
-    turns = [to_turn(which) for which in range(2)]
-    to_near(1, 1, turned)
-    for chunk in range(CHUNKS):
-        for which in range(2):
-            side = ways[which][0]
-            blk_copies[which, chunk].wait_recv()
-            if chunk in plain:
-                far_copies[side, chunk] = to_far(side, chunk)
-            to_near(side, 0, chunk)
-    for chunk in plain:
-        far_copies[1, chunk].wait_recv()
-        to_near(1, 1, chunk)
-    for which in range(2):
-        turns[which].wait_recv()
-        to_near(ways[which][0], 1, turned)
-    for chunk in plain:
-        for side in (0, 2):
-            far_copies[side, chunk].wait_recv()
-            to_near(side, 1, chunk)
+    def pair_came(member, chunk):
+        pair_copies[member, chunk].wait_recv()
+        to_onward(member, chunk)
+        if member == 0 and chunk in PLAIN:
+            to_far(2, chunk)
+        to_near(2, member, chunk)
+
+    def on_came(member, chunk):
+        on_copies[member, chunk].wait_recv()
+        if member == 0 and chunk in PLAIN:
+            to_far(0, chunk)
+        to_near(0, member, chunk)
+
+    def far_came(side, chunk):
+        far_copies[side, chunk].wait_recv()
+        if side == 1 and chunk in TURNED:
+            to_pair(1, chunk)
+        to_near(side, 1, chunk)
+
+    for own, over in zip(PLAIN, TURNED):
+        far_came(1, over)
+        pair_came(0, own)
+    for chunk in PLAIN:
+        on_came(0, chunk)
+    for chunk in TURNED:
+        pair_came(0, chunk)
+    for chunk in PLAIN:
+        far_came(1, chunk)
+    for chunk in TURNED:
+        pair_came(1, chunk)
+        on_came(0, chunk)
+    for chunk in PLAIN:
+        far_came(2, chunk)
+        far_came(0, chunk)
+    for chunk in TURNED:
+        on_came(1, chunk)
     for copy in near_copies:
         copy.wait_recv()
     for copy in started:
@@ -125,8 +147,9 @@
         in_specs=[VMEM],
         out_specs=VMEM,
         scratch_shapes=[
-            dma, dma((2, CHUNKS)), dma((2, CHUNKS)), dma((SIDES, CHUNKS)), dma((SIDES, CHUNKS)),
-            dma((SIDES, 2, CHUNKS)), dma((SIDES, 2, CHUNKS)), dma((2,)), dma((2,)),
+            dma, dma((2, CHUNKS)), dma((2, CHUNKS)), dma((2, CHUNKS)), dma((2, CHUNKS)),
+            dma((SIDES, CHUNKS)), dma((SIDES, CHUNKS)), dma((SIDES, 2, CHUNKS)),
+            dma((SIDES, 2, CHUNKS)),
         ],
         compiler_params=pltpu.CompilerParams(
             collective_id=0, has_side_effects=True, vmem_limit_bytes=LIMIT),
@@ -277,17 +300,16 @@
     )(counts, cols, window.reshape(window_shape), values, weight, bias.reshape(1, -1), out_grad)
 
 
-def reduce_kernel(count, terms, grads, out_ref, whole, near_buf, far_out, far_buf, blk_out,
-                  blk_buf, turn_buf, rep_buf, share_out, share_buf, summed, near_send, near_recv,
-                  far_send, far_recv, blk_send, blk_recv, turn_send, turn_recv, rep_send, rep_recv,
+def reduce_kernel(count, terms, grads, out_ref, whole, near_buf, far_out, far_buf, on_out, on_buf,
+                  pair_out, pair_buf, rep_buf, share_out, share_buf, summed, near_send, near_recv,
+                  far_send, far_recv, on_send, on_recv, pair_send, pair_recv, rep_send, rep_recv,
                   share_send, share_recv, back_send, back_recv, last_send, last_recv):
     blk, rep = lax.axis_index("blk"), lax.axis_index("rep")
     near, far = partners()
     across = (near + 2) % GROUP
-    before, after = (blk + count - 1) % count, (blk + 1) % count
+    pair, onward, behind, on_side, pair_side = lines(count)
+    sides = (on_side, 1, pair_side)
     step = out_ref.shape[0] // CHUNKS
-    turned = CHUNKS - 1
-    plain = range(CHUNKS - 1)
     f32 = jnp.float32
 
     barrier = pltpu.get_barrier_semaphore()
@@ -323,12 +345,11 @@
             for turn in range(1, count)
         ]
 
-    near_copies, far_copies, blk_copies, turn_copies = {}, {}, {}, {}
-    ways = ((0, before), (2, after))
+    near_copies, far_copies, on_copies, pair_copies = {}, {}, {}, {}
 
     def to_near(side, whose):
         near_copies[side, whose] = start(
-            terms.at[side, (near, across)[whose]], near_buf.at[side, whose],
+            terms.at[sides[side], (near, across)[whose]], near_buf.at[side, whose],
             near_send.at[side, whose], near_recv.at[side, whose], (blk, near))
 
     to_near(0, 1)
@@ -344,34 +365,37 @@
 
     def chip_sum(side, whose, chunk):
         part = here(chunk)
-        return (terms[side, (rep, far)[whose], part].astype(f32)
+        return (terms[sides[side], (rep, far)[whose], part].astype(f32)
                 + near_buf[side, whose, part].astype(f32))
 
+    def hand(copies, key, value, out, buf, send, recv, device):
+        where, part = key[0], here(key[1])
+        out[where, part] = value.astype(out.dtype)
+        copies[key] = start(
+            out.at[where, part], buf.at[where, part], send.at[key[0], key[1]],
+            recv.at[key[0], key[1]], device)
+
     def to_far(side, chunk, value):
-        part = here(chunk)
-        far_out[side, part] = value.astype(far_out.dtype)
-        far_copies[side, chunk] = start(
-            far_out.at[side, part], far_buf.at[side, part], far_send.at[side, chunk],
-            far_recv.at[side, chunk], (blk, far))
-
-    def to_blk(which, chunk, value):
-        part = here(chunk)
-        blk_out[which, part] = value.astype(blk_out.dtype)
-        blk_copies[which, chunk] = start(
-            blk_out.at[which, part], blk_buf.at[which, part], blk_send.at[which, chunk],
-            blk_recv.at[which, chunk], (ways[which][1], rep))
+        hand(far_copies, (side, chunk), value, far_out, far_buf, far_send, far_recv, (blk, far))
+
+    def to_behind(whose, chunk, value):
+        hand(on_copies, (whose, chunk), value, on_out, on_buf, on_send, on_recv, (behind, rep))
+
+    def to_pair(whose, chunk, value):
+        hand(pair_copies, (whose, chunk), value, pair_out, pair_buf, pair_send, pair_recv,
+             (pair, rep))
+
+    def came(copies, key, buf):
+        copies[key].wait_recv()
+        return buf[key[0], here(key[1])].astype(f32)
 
     near_copies[0, 1].wait_recv()
+    for over, chunk in zip(TURNED, PLAIN):
+        to_behind(1, over, chip_sum(0, 1, over))
+        to_far(0, chunk, chip_sum(0, 1, chunk))
     near_copies[2, 1].wait_recv()
-    for which, (side, block) in enumerate(ways):
-        part = here(turned)
-        far_out[side, part] = chip_sum(side, 1, turned).astype(far_out.dtype)
-        turn_copies[which] = start(
-            far_out.at[side, part], turn_buf.at[which], turn_send.at[which], turn_recv.at[which],
-            (block, rep))
-    for chunk in plain:
-        for side in (0, 2):
-            to_far(side, chunk, chip_sum(side, 1, chunk))
+    for chunk in PLAIN:
+        to_far(2, chunk, chip_sum(2, 1, chunk))
 
     for copy in rep_copies:
         copy.wait_recv()
@@ -388,32 +412,33 @@
         share_send, share_recv)
 
     near_copies[0, 0].wait_recv()
+    for chunk in TURNED:
+        to_behind(0, chunk, chip_sum(0, 0, chunk))
+    near_copies[1, 1].wait_recv()
+    for chunk in PLAIN:
+        to_far(1, chunk, chip_sum(1, 1, chunk))
+    for chunk in TURNED:
+        to_pair(1, chunk, chip_sum(2, 1, chunk) + came(on_copies, (1, chunk), on_buf))
+    for chunk in PLAIN:
+        to_behind(0, chunk, chip_sum(0, 0, chunk) + came(far_copies, (0, chunk), far_buf))
     near_copies[2, 0].wait_recv()
-    for which, (side, _) in enumerate(ways):
-        to_blk(which, turned, chip_sum(side, 0, turned))
-    near_copies[1, 1].wait_recv()
-    for chunk in plain:
-        to_far(1, chunk, chip_sum(1, 1, chunk))
-    own = chip_sum(1, 1, turned)
-    for which in range(2):
-        turn_copies[which].wait_recv()
-        own += turn_buf[which].astype(f32)
-    to_far(1, turned, own)
-
-    for chunk in plain:
-        for which, (side, _) in enumerate(ways):
-            far_copies[side, chunk].wait_recv()
-            to_blk(which, chunk,
-                   chip_sum(side, 0, chunk) + far_buf[side, here(chunk)].astype(f32))
-        if chunk == 0:
-            for copy in share_copies:
-                copy.wait_recv()
-            mine = share_out[blk]
-            for turn in range(1, count):
-                mine += share_buf[turn - 1]
-            summed[blk] = mine
-            back_copies = to_blks(
-                lambda turn: summed.at[blk], lambda turn: summed.at[blk], back_send, back_recv)
+    for chunk in TURNED:
+        to_pair(0, chunk, chip_sum(2, 0, chunk) + came(on_copies, (0, chunk), on_buf))
+    for chunk in TURNED:
+        to_far(1, chunk, chip_sum(1, 1, chunk) + came(pair_copies, (1, chunk), pair_buf))
+
+    for copy in share_copies:
+        copy.wait_recv()
+    mine = share_out[blk]
+    for turn in range(1, count):
+        mine += share_buf[turn - 1]
+    summed[blk] = mine
+    back_copies = to_blks(
+        lambda turn: summed.at[blk], lambda turn: summed.at[blk], back_send, back_recv)
+
+    for chunk in PLAIN:
+        to_pair(0, chunk, chip_sum(2, 0, chunk) + came(far_copies, (2, chunk), far_buf)
+                + came(on_copies, (0, chunk), on_buf))
 
     for copy in back_copies:
         copy.wait_recv()
@@ -424,15 +449,10 @@
         lambda turn: whole.at[rep], lambda turn: whole.at[rep], last_send, last_recv)
 
     near_copies[1, 0].wait_recv()
-    for chunk in (turned, *plain):
-        part = here(chunk)
-        for which in range(2):
-            blk_copies[which, chunk].wait_recv()
-        far_copies[1, chunk].wait_recv()
-        total = chip_sum(1, 0, chunk) + far_buf[1, part].astype(f32)
-        for which in range(2):
-            total += blk_buf[which, part].astype(f32)
-        out_ref[part] = total
+    for chunk in TURNED + PLAIN:
+        out_ref[here(chunk)] = (
+            chip_sum(1, 0, chunk) + came(far_copies, (1, chunk), far_buf)
+            + came(pair_copies, (0, chunk), pair_buf))
 
     for copy in last_copies:
         copy.wait_recv()
@@ -449,7 +469,7 @@
     share = in_dim // count + SUM_ROWS
     piece = (tiles, in_dim, TILE)
     dma = pltpu.SemaphoreType.DMA
-    pairs = [(SIDES, 2), (SIDES, CHUNKS), (2, CHUNKS), (2,), (GROUP - 1,), (count - 1,),
+    pairs = [(SIDES, 2), (SIDES, CHUNKS), (2, CHUNKS), (2, CHUNKS), (GROUP - 1,), (count - 1,),
              (count - 1,), (GROUP - 1,)]
     return pl.pallas_call(
         functools.partial(reduce_kernel, count),
@@ -465,7 +485,8 @@
             pltpu.VMEM((SIDES,) + piece, jnp.bfloat16),
             pltpu.VMEM((2,) + piece, jnp.bfloat16),
             pltpu.VMEM((2,) + piece, jnp.bfloat16),
-            pltpu.VMEM((2, tiles // CHUNKS) + piece[1:], jnp.bfloat16),
+            pltpu.VMEM((2,) + piece, jnp.bfloat16),
+            pltpu.VMEM((2,) + piece, jnp.bfloat16),
             pltpu.VMEM((GROUP - 1,) + grads.shape[1:], jnp.bfloat16),
             pltpu.VMEM((count, share, cut), jnp.float32),
             pltpu.VMEM((count - 1, share, cut), jnp.float32),

time: 80.5 us -> 81.4 us (1.011)
  Pallas kernels: 79.4 us -> 80.8 us
    pallas_call x1, Pallas kernels: 26.4 us -> 33.6 us  [reduce(): pl.pallas_call(functools.partial(reduce_kernel, count), out_shape=(jax.Sh...]
    pallas_call x1, Pallas kernels: 24.5 us -> 20.4 us  [layer(): pl.pallas_call(functools.partial(layer_kernel, factor), out_shape=(jax.Sh...]
    pallas_call x1, Pallas kernels: 26.3 us -> 24.7 us  [gather(): pl.pallas_call(functools.partial(gather_kernel, lax.axis_size('blk')), ou...]
where the time goes in v3:
time: 81.4 us; the launch traced here: 81.5 us
  Pallas kernels  80.8 us (99%)
    pallas_call x1, Pallas kernels, reduce(): pl.pallas_call(functools.partial(reduce_kernel, count), out_shape=(jax.Sh...  33.6 us
    pallas_call x1, Pallas kernels, gather(): pl.pallas_call(functools.partial(gather_kernel, lax.axis_size('blk')), ou...  24.7 us
    pallas_call x1, Pallas kernels, layer(): pl.pallas_call(functools.partial(layer_kernel, factor), out_shape=(jax.Sh...  20.4 us
    pallas_call x1, Pallas kernels, finish(): pl.pallas_call(finish_kernel, out_shape=(jax.ShapeDtypeStruct((tiles * TI...  2.09 us

profile of v3, /device:TPU:0, one launch (start us, length us, event | category | flops | bytes accessed | tf_op | source)
XLA Modules:
  0.0 81.5 jit_solution(15468209030131877469)
XLA Ops:
  0.6 24.7 %gather_window.1 = bf16[3,4,1024,128]{3,2,1,0:T(8,128)(2,1)} custom-call(bf16[1024,128]{1,0:T(8,128)(2,1)} %own_ref.1), custom_call_target="tpu_custom_call" | custom-call | tf_op jit(solution)/shard_map/gather_window/pallas_call | solution.py:144
  25.3 20.4 %layer.1 = (bf16[1024,512]{1,0:T(8,128)(2,1)}, bf16[96,128,128]{2,1,0:T(8,128)(2,1)}, bf16[4,144,128]{2,1,0:T(8,128)(2,1)}) custom-call(s32[8]{0:T(128)} %counts.1, s32[8,32]{1,0:T(8,128)} %cols.1, bf16[96,128,128]{2,1,0:T(8,128)(2,1)} %bitcast.4, bf16[1024,4096]{1,0:T(8,128)(2,1)} %val_hbm.1, bf16[128,512]{1,0:T(8,128)(2,1)} %weight.1, f32[1,512]{1,0:T(1,128)} %bitcast.6, ...), custom_call_target="tpu_custom_call" | custom-call | tf_op jit(solution)/shard_map/layer/pallas_call | solution.py:277
  45.7 33.6 %reduce_terms.1 = (f32[8,128,128]{2,1,0:T(8,128)}, bf16[4,144,128]{2,1,0:T(8,128)(2,1)}) custom-call(bf16[3,4,8,128,128]{4,3,2,1,0:T(8,128)(2,1)} %bitcast.5, bf16[4,144,128]{2,1,0:T(8,128)(2,1)} %get-tuple-element.14.grads), custom_call_target="tpu_custom_call" | custom-call | tf_op jit(solution)/shard_map/reduce_terms/pallas_call | solution.py:474
  79.4 2.1 %finish.1 = (f32[1024,128]{1,0:T(8,128)}, f32[128,512]{1,0:T(8,128)}, f32[1,512]{1,0:T(1,128)}) custom-call(f32[8,128,128]{2,1,0:T(8,128)} %get-tuple-element.15.turned, bf16[4,144,128]{2,1,0:T(8,128)(2,1)} %get-tuple-element.16.whole), custom_call_target="tpu_custom_call" | custom-call | tf_op jit(solution)/shard_map/finish/pallas_call | solution.py:514

commit v4 on v3

--- a/solution.py
+++ b/solution.py
@@ -14,6 +14,7 @@
 CHUNKS = 4
 PLAIN = (0, 1)
 TURNED = (2, 3)
+DENSE = 2
 SPAN = 8
 BIAS_ROWS = 16
 SUM_ROWS = 8
@@ -169,8 +170,8 @@
 
 
 def layer_kernel(factor, counts, cols, win_hbm, val_hbm, weight, bias, og_hbm, act_out, terms_out,
-                 grad_out, vals, win, og, placed, agg, pre_grad, row_grad, acc, bias_sum, val_sem,
-                 win_sem, og_sem):
+                 grad_out, vals, win, og, placed, agg, pre_grad, row_grad, acc, bias_sum, rounded,
+                 val_sem, win_sem, og_sem, out_sem):
     tiles, _, wide = vals.shape
     spans = wide // (SPAN * TILE)
     win_copy = pltpu.make_async_copy(win_hbm, win, win_sem)
@@ -214,21 +215,25 @@
     og_copy.wait()
     bias_sum[...] = jnp.zeros_like(bias_sum)
 
+    taken = DENSE * TILE
+
     def dense(t, carry):
-        here = pl.ds(pl.multiple_of(t * TILE, TILE), TILE)
+        here = pl.ds(pl.multiple_of(t * taken, taken), taken)
         pre_act = jnp.dot(agg[here], weight[...], preferred_element_type=jnp.float32) + bias[...]
         value_part, slope = gelu_parts(pre_act)
         act_out[here] = value_part.astype(act_out.dtype)
         grad = (og[here].astype(jnp.float32) * slope).astype(jnp.bfloat16)
         pre_grad[here] = grad
         bias_sum[...] += jnp.sum(
-            grad.astype(jnp.float32).reshape(TILE // 8, 8, grad.shape[1]), axis=0)
-        row_grad[t] = lax.dot_general(
+            grad.astype(jnp.float32).reshape(taken // 8, 8, grad.shape[1]), axis=0)
+        turned = lax.dot_general(
             weight[...], grad, (((1,), (1,)), ((), ())), preferred_element_type=jnp.float32
         ).astype(row_grad.dtype)
+        for k in range(DENSE):
+            row_grad[t * DENSE + k] = turned[:, k * TILE:(k + 1) * TILE]
         return carry
 
-    lax.fori_loop(0, tiles, dense, 0)
+    lax.fori_loop(0, tiles // DENSE, dense, 0)
     weight_grad = lax.dot_general(
         agg[...], pre_grad[...], (((0,), (0,)), ((), ())), preferred_element_type=jnp.float32
     ) * factor
@@ -259,11 +264,17 @@
 
     lax.fori_loop(0, tiles, backward, 0)
 
-    def hand_on(w, carry):
-        terms_out[w] = placed[w].astype(terms_out.dtype)
-        return carry
-
-    lax.fori_loop(0, placed.shape[0], hand_on, 0)
+    def out_copy(piece):
+        here = pl.ds(piece * tiles, tiles)
+        return pltpu.make_async_copy(rounded.at[here], terms_out.at[here], out_sem.at[piece])
+
+    pieces = placed.shape[0] // tiles
+    for piece in range(pieces):
+        here = pl.ds(piece * tiles, tiles)
+        rounded[here] = placed[here].astype(rounded.dtype)
+        out_copy(piece).start()
+    for piece in range(pieces):
+        out_copy(piece).wait()
 
 
 def layer(counts, cols, window, values, weight, bias, out_grad, factor):
@@ -282,7 +293,7 @@
             jax.ShapeDtypeStruct(grad_shape, jnp.bfloat16),
         ),
         in_specs=[SMEM, SMEM, ANY, ANY, VMEM, VMEM, ANY],
-        out_specs=(VMEM, VMEM, VMEM),
+        out_specs=(VMEM, ANY, VMEM),
         scratch_shapes=[
             pltpu.VMEM((tiles, TILE, wide), jnp.bfloat16),
             pltpu.VMEM(window_shape, jnp.bfloat16),
@@ -293,23 +304,25 @@
             pltpu.VMEM((tiles, in_dim, TILE), jnp.bfloat16),
             pltpu.VMEM((TILE, in_dim), jnp.float32),
             pltpu.VMEM((8, out_dim), jnp.float32),
-            dma((tiles,)), dma, dma,
+            pltpu.VMEM((window_tiles, in_dim, TILE), jnp.bfloat16),
+            dma((tiles,)), dma, dma, dma((SIDES * GROUP,)),
         ],
         compiler_params=pltpu.CompilerParams(vmem_limit_bytes=LIMIT),
         name="layer",
     )(counts, cols, window.reshape(window_shape), values, weight, bias.reshape(1, -1), out_grad)
 
 
-def reduce_kernel(count, terms, grads, out_ref, whole, near_buf, far_out, far_buf, on_out, on_buf,
-                  pair_out, pair_buf, rep_buf, share_out, share_buf, summed, near_send, near_recv,
-                  far_send, far_recv, on_send, on_recv, pair_send, pair_recv, rep_send, rep_recv,
+def reduce_kernel(count, terms, grads, out_ref, whole, near_buf, far_out, far_buf, blk_out,
+                  blk_buf, turn_buf, rep_buf, share_out, share_buf, summed, near_send, near_recv,
+                  far_send, far_recv, blk_send, blk_recv, turn_send, turn_recv, rep_send, rep_recv,
                   share_send, share_recv, back_send, back_recv, last_send, last_recv):
     blk, rep = lax.axis_index("blk"), lax.axis_index("rep")
     near, far = partners()
     across = (near + 2) % GROUP
-    pair, onward, behind, on_side, pair_side = lines(count)
-    sides = (on_side, 1, pair_side)
+    before, after = (blk + count - 1) % count, (blk + 1) % count
     step = out_ref.shape[0] // CHUNKS
+    turned = CHUNKS - 1
+    plain = range(CHUNKS - 1)
     f32 = jnp.float32
 
     barrier = pltpu.get_barrier_semaphore()
@@ -345,11 +358,12 @@
             for turn in range(1, count)
         ]
 
-    near_copies, far_copies, on_copies, pair_copies = {}, {}, {}, {}
+    near_copies, far_copies, blk_copies, turn_copies = {}, {}, {}, {}
+    ways = ((0, before), (2, after))
 
     def to_near(side, whose):
         near_copies[side, whose] = start(
-            terms.at[sides[side], (near, across)[whose]], near_buf.at[side, whose],
+            terms.at[side, (near, across)[whose]], near_buf.at[side, whose],
             near_send.at[side, whose], near_recv.at[side, whose], (blk, near))
 
     to_near(0, 1)
@@ -365,37 +379,34 @@
 
     def chip_sum(side, whose, chunk):
         part = here(chunk)
-        return (terms[sides[side], (rep, far)[whose], part].astype(f32)
+        return (terms[side, (rep, far)[whose], part].astype(f32)
                 + near_buf[side, whose, part].astype(f32))
 
-    def hand(copies, key, value, out, buf, send, recv, device):
-        where, part = key[0], here(key[1])
-        out[where, part] = value.astype(out.dtype)
-        copies[key] = start(
-            out.at[where, part], buf.at[where, part], send.at[key[0], key[1]],
-            recv.at[key[0], key[1]], device)
-
     def to_far(side, chunk, value):
-        hand(far_copies, (side, chunk), value, far_out, far_buf, far_send, far_recv, (blk, far))
-
-    def to_behind(whose, chunk, value):
-        hand(on_copies, (whose, chunk), value, on_out, on_buf, on_send, on_recv, (behind, rep))
-
-    def to_pair(whose, chunk, value):
-        hand(pair_copies, (whose, chunk), value, pair_out, pair_buf, pair_send, pair_recv,
-             (pair, rep))
-
-    def came(copies, key, buf):
-        copies[key].wait_recv()
-        return buf[key[0], here(key[1])].astype(f32)
+        part = here(chunk)
+        far_out[side, part] = value.astype(far_out.dtype)
+        far_copies[side, chunk] = start(
+            far_out.at[side, part], far_buf.at[side, part], far_send.at[side, chunk],
+            far_recv.at[side, chunk], (blk, far))
+
+    def to_blk(which, chunk, value):
+        part = here(chunk)
+        blk_out[which, part] = value.astype(blk_out.dtype)
+        blk_copies[which, chunk] = start(
+            blk_out.at[which, part], blk_buf.at[which, part], blk_send.at[which, chunk],
+            blk_recv.at[which, chunk], (ways[which][1], rep))
 
     near_copies[0, 1].wait_recv()
-    for over, chunk in zip(TURNED, PLAIN):
-        to_behind(1, over, chip_sum(0, 1, over))
-        to_far(0, chunk, chip_sum(0, 1, chunk))
     near_copies[2, 1].wait_recv()
-    for chunk in PLAIN:
-        to_far(2, chunk, chip_sum(2, 1, chunk))
+    for which, (side, block) in enumerate(ways):
+        part = here(turned)
+        far_out[side, part] = chip_sum(side, 1, turned).astype(far_out.dtype)
+        turn_copies[which] = start(
+            far_out.at[side, part], turn_buf.at[which], turn_send.at[which], turn_recv.at[which],
+            (block, rep))
+    for chunk in plain:
+        for side in (0, 2):
+            to_far(side, chunk, chip_sum(side, 1, chunk))
 
     for copy in rep_copies:
         copy.wait_recv()
@@ -412,33 +423,32 @@
         share_send, share_recv)
 
     near_copies[0, 0].wait_recv()
-    for chunk in TURNED:
-        to_behind(0, chunk, chip_sum(0, 0, chunk))
+    near_copies[2, 0].wait_recv()
+    for which, (side, _) in enumerate(ways):
+        to_blk(which, turned, chip_sum(side, 0, turned))
     near_copies[1, 1].wait_recv()
-    for chunk in PLAIN:
+    for chunk in plain:
         to_far(1, chunk, chip_sum(1, 1, chunk))
-    for chunk in TURNED:
-        to_pair(1, chunk, chip_sum(2, 1, chunk) + came(on_copies, (1, chunk), on_buf))
-    for chunk in PLAIN:
-        to_behind(0, chunk, chip_sum(0, 0, chunk) + came(far_copies, (0, chunk), far_buf))
-    near_copies[2, 0].wait_recv()
-    for chunk in TURNED:
-        to_pair(0, chunk, chip_sum(2, 0, chunk) + came(on_copies, (0, chunk), on_buf))
-    for chunk in TURNED:
-        to_far(1, chunk, chip_sum(1, 1, chunk) + came(pair_copies, (1, chunk), pair_buf))
-
-    for copy in share_copies:
-        copy.wait_recv()
-    mine = share_out[blk]
-    for turn in range(1, count):
-        mine += share_buf[turn - 1]
-    summed[blk] = mine
-    back_copies = to_blks(
-        lambda turn: summed.at[blk], lambda turn: summed.at[blk], back_send, back_recv)
-
-    for chunk in PLAIN:
-        to_pair(0, chunk, chip_sum(2, 0, chunk) + came(far_copies, (2, chunk), far_buf)
-                + came(on_copies, (0, chunk), on_buf))
+    own = chip_sum(1, 1, turned)
+    for which in range(2):
+        turn_copies[which].wait_recv()
+        own += turn_buf[which].astype(f32)
+    to_far(1, turned, own)
+
+    for chunk in plain:
+        for which, (side, _) in enumerate(ways):
+            far_copies[side, chunk].wait_recv()
+            to_blk(which, chunk,
+                   chip_sum(side, 0, chunk) + far_buf[side, here(chunk)].astype(f32))
+        if chunk == 0:
+            for copy in share_copies:
+                copy.wait_recv()
+            mine = share_out[blk]
+            for turn in range(1, count):
+                mine += share_buf[turn - 1]
+            summed[blk] = mine
+            back_copies = to_blks(
+                lambda turn: summed.at[blk], lambda turn: summed.at[blk], back_send, back_recv)
 
     for copy in back_copies:
         copy.wait_recv()
@@ -449,10 +459,15 @@
         lambda turn: whole.at[rep], lambda turn: whole.at[rep], last_send, last_recv)
 
     near_copies[1, 0].wait_recv()
-    for chunk in TURNED + PLAIN:
-        out_ref[here(chunk)] = (
-            chip_sum(1, 0, chunk) + came(far_copies, (1, chunk), far_buf)
-            + came(pair_copies, (0, chunk), pair_buf))
+    for chunk in (turned, *plain):
+        part = here(chunk)
+        for which in range(2):
+            blk_copies[which, chunk].wait_recv()
+        far_copies[1, chunk].wait_recv()
+        total = chip_sum(1, 0, chunk) + far_buf[1, part].astype(f32)
+        for which in range(2):
+            total += blk_buf[which, part].astype(f32)
+        out_ref[part] = total
 
     for copy in last_copies:
         copy.wait_recv()
@@ -469,7 +484,7 @@
     share = in_dim // count + SUM_ROWS
     piece = (tiles, in_dim, TILE)
     dma = pltpu.SemaphoreType.DMA
-    pairs = [(SIDES, 2), (SIDES, CHUNKS), (2, CHUNKS), (2, CHUNKS), (GROUP - 1,), (count - 1,),
+    pairs = [(SIDES, 2), (SIDES, CHUNKS), (2, CHUNKS), (2,), (GROUP - 1,), (count - 1,),
              (count - 1,), (GROUP - 1,)]
     return pl.pallas_call(
         functools.partial(reduce_kernel, count),
@@ -485,8 +500,7 @@
             pltpu.VMEM((SIDES,) + piece, jnp.bfloat16),
             pltpu.VMEM((2,) + piece, jnp.bfloat16),
             pltpu.VMEM((2,) + piece, jnp.bfloat16),
-            pltpu.VMEM((2,) + piece, jnp.bfloat16),
-            pltpu.VMEM((2,) + piece, jnp.bfloat16),
+            pltpu.VMEM((2, tiles // CHUNKS) + piece[1:], jnp.bfloat16),
             pltpu.VMEM((GROUP - 1,) + grads.shape[1:], jnp.bfloat16),
             pltpu.VMEM((count, share, cut), jnp.float32),
             pltpu.VMEM((count - 1, share, cut), jnp.float32),

time: 81.4 us -> 77.2 us (0.948)
  Pallas kernels: 80.8 us -> 76 us
    pallas_call x1, Pallas kernels: 33.6 us -> 28.1 us  [reduce(): pl.pallas_call(functools.partial(reduce_kernel, count), out_shape=(jax.Sh...]
where the time goes in v4:
time: 77.2 us; the launch traced here: 76.6 us
  Pallas kernels  76 us (98%)
    pallas_call x1, Pallas kernels, reduce(): pl.pallas_call(functools.partial(reduce_kernel, count), out_shape=(jax.Sh...  28.1 us
    pallas_call x1, Pallas kernels, gather(): pl.pallas_call(functools.partial(gather_kernel, lax.axis_size('blk')), ou...  24.7 us
    pallas_call x1, Pallas kernels, layer(): pl.pallas_call(functools.partial(layer_kernel, factor), out_shape=(jax.Sh...  21.1 us
    pallas_call x1, Pallas kernels, finish(): pl.pallas_call(finish_kernel, out_shape=(jax.ShapeDtypeStruct((tiles * TI...  2.09 us

profile of v4, /device:TPU:0, one launch (start us, length us, event | category | flops | bytes accessed | tf_op | source)
XLA Modules:
  0.0 76.6 jit_solution(3985250942844725214)
XLA Ops:
  0.6 24.7 %gather_window.1 = bf16[3,4,1024,128]{3,2,1,0:T(8,128)(2,1)} custom-call(bf16[1024,128]{1,0:T(8,128)(2,1)} %own_ref.1), custom_call_target="tpu_custom_call" | custom-call | tf_op jit(solution)/shard_map/gather_window/pallas_call | solution.py:145
  25.3 21.1 %layer.1 = (bf16[1024,512]{1,0:T(8,128)(2,1)}, bf16[96,128,128]{2,1,0:T(8,128)(2,1)}, bf16[4,144,128]{2,1,0:T(8,128)(2,1)}) custom-call(s32[8]{0:T(128)} %counts.1, s32[8,32]{1,0:T(8,128)} %cols.1, bf16[96,128,128]{2,1,0:T(8,128)(2,1)} %bitcast.4, bf16[1024,4096]{1,0:T(8,128)(2,1)} %val_hbm.1, bf16[128,512]{1,0:T(8,128)(2,1)} %weight.1, f32[1,512]{1,0:T(1,128)} %bitcast.6, ...), custom_call_target="tpu_custom_call" | custom-call | tf_op jit(solution)/shard_map/layer/pallas_call | solution.py:288
  46.5 28.1 %reduce_terms.1 = (f32[8,128,128]{2,1,0:T(8,128)}, bf16[4,144,128]{2,1,0:T(8,128)(2,1)}) custom-call(bf16[3,4,8,128,128]{4,3,2,1,0:T(8,128)(2,1)} %bitcast.5, bf16[4,144,128]{2,1,0:T(8,128)(2,1)} %get-tuple-element.14.grads), custom_call_target="tpu_custom_call" | custom-call | tf_op jit(solution)/shard_map/reduce_terms/pallas_call | solution.py:489
  74.5 2.1 %finish.1 = (f32[1024,128]{1,0:T(8,128)}, f32[128,512]{1,0:T(8,128)}, f32[1,512]{1,0:T(1,128)}) custom-call(f32[8,128,128]{2,1,0:T(8,128)} %get-tuple-element.15.turned, bf16[4,144,128]{2,1,0:T(8,128)(2,1)} %get-tuple-element.16.whole), custom_call_target="tpu_custom_call" | custom-call | tf_op jit(solution)/shard_map/finish/pallas_call | solution.py:528
